TPU v7x, 128 devices: a whole 4x4x4 slice. The times are simulated.
128 devices in a mesh: chan: 4 (over x), blk: 32 (over z, y, core).
Axes of the slice: x: 4, y: 4, z: 4, core: 2. Of those that a mesh axis runs over, the one named last changes fastest.
Arguments:
- coeffs: bfloat16 [12, 2, 3072, 1536], P('chan', None, 'blk'), may hold values from -0.15 to 0.15
- legendre: bfloat16 [4, 768, 256, 1536], P('chan', 'blk'), may hold values from -0.15625 to 0.15625
- m_order: int32 [3072], replicated, may hold values from 0 to 3071, as said below
- sector_len: int32 [512, 16], P(('chan', 'blk')), may hold values from 256 to 4352, as said below
Outputs:
- ilc_map: float32 [512, 8192], P(('chan', 'blk'))
Inputs may be any that keep to these rules, and one draw needn't show every extreme that they name: `m_order`: a permutation of 0 to 3071; slots 2 j and 2 j + 1 hold the orders m and 3071 - m. `sector_len`: the 16 lengths of each cycle sum to 8192.
All inputs are finite; a program needn't handle non-finite values.
Results may differ from a plain program's by a relative error of at most 0.0003.
Values may be sent and summed in bfloat16 or wider, within the bound.
No kernel may reach another device: no remote copies, remote signals or barrier semaphores. Data moves between devices by JAX's collectives and lax.ppermute only.
A program may use at most 256 MiB of HBM per device.

v0:
```python
import functools

import jax
import jax.numpy as jnp
import ml_dtypes
import numpy as np
from jax import lax
from jax.experimental import pallas as pl
from jax.experimental.pallas import tpu as pltpu
from jax.sharding import PartitionSpec as P

M = 3072
LB = 1536
PIX = 8192
CH = 12
NSEC = 16
NSLOT = 24
NCYC = 4
N_CHAN = 4
N_BLK = 32
N_DEV = N_CHAN * N_BLK
RIDGE_FACTOR = 0.05

NA, NB, NM1, NM2 = 128, 64, 128, 24
ROWS = 18

f32, bf16 = jnp.float32, jnp.bfloat16


def split_np(x):
    high = x.astype(ml_dtypes.bfloat16)
    low = (x - high.astype(np.float64)).astype(ml_dtypes.bfloat16)
    return high, low


@functools.cache
def tables():
    b, m2 = np.arange(NB)[:, None], np.arange(NM2)[None, :]
    angle = 2 * np.pi * ((b * m2) % 64) / 64
    stage1 = np.block([[np.cos(angle), -np.sin(angle)], [np.sin(angle), np.cos(angle)]])
    high, low = split_np(stage1)
    stage1 = np.concatenate([high, high, low], axis=1)
    m1 = np.arange(NM1)[None, :]
    angle = 2 * np.pi * b * m1 / PIX
    twiddle = np.concatenate([np.cos(angle), np.sin(angle)], axis=0).astype(np.float32)
    m1, a = np.arange(NM1)[:, None], np.arange(NA)[None, :]
    angle = 2 * np.pi * ((m1 * a) % 128) / 128
    stage2 = 2.0 * np.concatenate([np.cos(angle), -np.sin(angle)], axis=0)
    stage2 = np.concatenate(split_np(stage2), axis=1)
    return stage1, twiddle, stage2


def split2(x):
    high = x.astype(bf16)
    return high, (x - high.astype(f32)).astype(bf16)


def split3(x):
    high = x.astype(bf16)
    rest = x - high.astype(f32)
    mid = rest.astype(bf16)
    return high, mid, (rest - mid.astype(f32)).astype(bf16)


def dot_nn(x, y):
    return lax.dot_general(x, y, (((1,), (0,)), ((), ())), preferred_element_type=f32)


def dot_nt(x, y):
    return lax.dot_general(x, y, (((1,), (1,)), ((), ())), preferred_element_type=f32)


def legendre_kernel(orders_ref, coef_ref, leg_ref, out_ref, wide_ref, acc_ref):
    step = pl.program_id(0)

    @pl.when(step == 0)
    def _():
        def widen(i, carry):
            value = coef_ref[i].astype(f32)
            for j in range(LB // 128):
                wide_ref[j, pl.ds(i * NSLOT, NSLOT), :] = value[:, j * 128 : (j + 1) * 128]
            return carry

        lax.fori_loop(0, 2 * CH, widen, 0)

    degree = (M - LB) + lax.broadcasted_iota(jnp.int32, (1, LB), 1)
    lane = lax.broadcasted_iota(jnp.int32, (64, 128), 1)
    half = lane < 64
    even_group = (lane & 32) == 0
    spare = (lane & 31) >= 24
    north, south = [], []
    for u in range(4):
        slot = step * 4 + u
        m = orders_ref[slot]
        coef = jnp.concatenate([wide_ref[j, pl.ds(slot, 2 * CH, stride=NSLOT), :] for j in range(LB // 128)], axis=1)
        keep = (degree >= m).astype(f32)
        sign = (1 - 2 * ((degree + m) & 1)).astype(f32) * keep
        none = jnp.zeros((8, LB), f32)
        up = jnp.concatenate([coef * keep, none], axis=0).astype(bf16)
        down = jnp.concatenate([coef * sign, none], axis=0).astype(bf16)
        rhs = jnp.concatenate([up, up, down, down], axis=0)
        acc_ref[u] = dot_nt(leg_ref[u], rhs)
        k0, k1, k2, k3 = (acc_ref[u, pl.ds(k, 64, stride=4), :] for k in range(4))
        first = jnp.where(even_group, k0, k1)
        second = jnp.where(even_group, k2, k3)
        north.append(jnp.where(half, first, pltpu.roll(second, 64, 1)))
        south.append(jnp.where(half, pltpu.roll(first, 64, 1), second))
    for hemi, part in enumerate((north, south)):
        for r in range(3):
            row = jnp.where(spare, pltpu.roll(part[3], 24 - 8 * r, 1), part[r])
            out_ref[pl.ds(hemi * 64 * ROWS + 3 * step + r, 64, stride=ROWS), :] = row


def legendre_call(orders, coef, legendre):
    return pl.pallas_call(
        legendre_kernel,
        out_shape=jax.ShapeDtypeStruct((N_DEV * ROWS, 128), f32),
        grid=(NSLOT // 4,),
        in_specs=[
            pl.BlockSpec(memory_space=pltpu.SMEM),
            pl.BlockSpec((2 * CH, NSLOT, LB), lambda i: (0, 0, 0)),
            pl.BlockSpec((4, 256, LB), lambda i: (i, 0, 0)),
        ],
        out_specs=pl.BlockSpec((N_DEV * ROWS, 128), lambda i: (0, 0)),
        scratch_shapes=[
            pltpu.VMEM((LB // 128, 2 * CH * NSLOT, 128), f32),
            pltpu.VMEM((4, 256, 128), f32),
        ],
        compiler_params=pltpu.CompilerParams(vmem_limit_bytes=40 * 2**20),
    )(orders, coef, legendre)


def map_kernel(
    orders_ref, lens_ref, data_ref, lane_len_ref, stage1_ref, twiddle_ref, stage2_ref, out_ref,
    last_ref, place_ref, turned_ref, map_ref, low_ref, high_ref, hot_ref, cov_ref, comb_ref, final_ref,
):
    lane = lax.broadcasted_iota(jnp.int32, (8, 128), 1)
    group = (lane & 31) >> 3

    def gather_last(i, carry):
        rows = [data_ref[pl.ds(i * 192 + r, 64, stride=3), :] for r in range(3)]
        wide = lax.broadcasted_iota(jnp.int32, (64, 128), 1)
        which = (wide & 31) >> 3
        rolled = [pltpu.roll(rows[r], 128 - (24 - 8 * r), 1) for r in range(3)]
        value = jnp.where(which == 0, rolled[0], jnp.where(which == 1, rolled[1], rolled[2]))
        last_ref[pl.ds(pl.multiple_of(i * 64, 64), 64), :] = value
        return carry

    lax.fori_loop(0, 12, gather_last, 0)

    def place(src, carry):
        base = ((src & (N_BLK - 1)) * N_CHAN + (src >> 5)) * NSLOT
        for t in range(6):
            for r in range(3):
                m = orders_ref[base + 4 * t + r]
                place_ref[pl.ds(m, 1), :] = data_ref[pl.ds(src * ROWS + 3 * t + r, 1), :]
            m = orders_ref[base + 4 * t + 3]
            place_ref[pl.ds(m, 1), :] = last_ref[pl.ds(src * 6 + t, 1), :]
        return carry

    lax.fori_loop(0, N_DEV, place, 0)
    place_ref[0:1, :] = place_ref[0:1, :] * 0.5

    for m2 in range(NM2):
        block = place_ref[m2 * 128 : (m2 + 1) * 128, :].T
        for k in range(NCYC):
            turned_ref[pl.ds(k * 2 * CH * NM2 + m2, 2 * CH, stride=NM2), :] = block[k * 32 : k * 32 + 24]

    stage1 = stage1_ref[...]

    def transform(i, carry):
        parts = []
        for j in range(2):
            high, low = split2(turned_ref[pl.ds(pl.multiple_of(i * 96 + j * 48, 16), 48), :])
            parts.append(jnp.concatenate([high, low, high], axis=0))
        inner = dot_nn(stage1, jnp.concatenate(parts, axis=1))
        tc, ts = twiddle_ref[0:64, :], twiddle_ref[64:128, :]
        outer = []
        for j in range(2):
            re, im = inner[0:64, j * 128 : (j + 1) * 128], inner[64:128, j * 128 : (j + 1) * 128]
            outer.append(jnp.concatenate([re * tc - im * ts, re * ts + im * tc], axis=1))
        high, low = split2(jnp.concatenate(outer, axis=0))
        both = dot_nn(high, stage2_ref[...])
        maps = both[:, 0:128] + (both[:, 128:256] + dot_nn(low, stage2_ref[:, 0:128]))
        map_ref[pl.ds(pl.multiple_of(i * 128, 128), 128), :] = maps
        return carry

    lax.fori_loop(0, NCYC * CH // 2, transform, 0)

    chunk = lax.broadcasted_iota(jnp.int32, (64, 128), 1)
    offset = lax.broadcasted_iota(jnp.int32, (64, 128), 0)
    low_ref[...] = jnp.zeros_like(low_ref)
    high_ref[...] = jnp.zeros_like(high_ref)
    cov_ref[...] = jnp.zeros_like(cov_ref)

    def sectors(k):
        start = chunk * 64
        which = jnp.zeros((64, 128), jnp.int32)
        bound = jnp.full((64, 128), PIX, jnp.int32)
        end = jnp.int32(0)
        for q in range(NSEC):
            end = end + lens_ref[k, q]
            passed = end <= start
            which = which + passed.astype(jnp.int32)
            bound = jnp.minimum(bound, jnp.where(passed, PIX, end))
        return which, start + offset < bound

    def moments(k, carry):
        which, inside = sectors(k)
        row = lax.broadcasted_iota(jnp.int32, (64, 128), 0)
        own = (row >> 4) == k
        hot_low = (own & ((row & 15) == which)).astype(bf16)
        hot_high = (own & ((row & 15) == which + 1)).astype(bf16)
        hot_ref[pl.ds(pl.multiple_of(k * 128, 128), 64), :] = hot_low
        hot_ref[pl.ds(pl.multiple_of(k * 128 + 64, 64), 64), :] = hot_high
        base = pl.multiple_of(k * CH * 64, 64)
        for i in range(CH):
            value = map_ref[pl.ds(base + i * 64, 64), :]
            low = jnp.where(inside, value, 0.0)
            high = jnp.where(inside, 0.0, value)
            for j in range(i, CH):
                other = map_ref[pl.ds(base + j * 64, 64), :]
                for part, ref in ((low, low_ref), (high, high_ref)):
                    total = jnp.sum(part * other, axis=0, keepdims=True)
                    ref[i * 16 + j : i * 16 + j + 1, :] = total
                    if i != j:
                        ref[j * 16 + i : j * 16 + i + 1, :] = total
        total = cov_ref[...]
        for ref, hot in ((low_ref, hot_low), (high_ref, hot_high)):
            for part in split3(ref[...]):
                total = total + dot_nt(part, hot)
        cov_ref[...] = total
        return carry

    lax.fori_loop(0, NCYC, moments, 0)

    scale = 1.0 / lane_len_ref[...].astype(f32)
    sub = lax.broadcasted_iota(jnp.int32, (16, 64), 0)
    mat = [cov_ref[i * 16 : (i + 1) * 16, :] * scale for i in range(CH)]
    trace = mat[0][0:1]
    for i in range(1, CH):
        trace = trace + mat[i][i : i + 1]
    ridge = trace * (RIDGE_FACTOR / CH)
    for i in range(CH):
        mat[i] = jnp.where(sub == CH, 1.0, jnp.where(sub == i, mat[i] + ridge, mat[i]))
    for p in range(CH):
        pivot = mat[p] / mat[p][p : p + 1]
        for i in range(CH):
            mat[i] = pivot if i == p else mat[i] - mat[i][p : p + 1] * pivot
    solved = [mat[i][CH : CH + 1] for i in range(CH)]
    norm = solved[0]
    for i in range(1, CH):
        norm = norm + solved[i]
    weights = jnp.concatenate([s / norm for s in solved] + [jnp.zeros((4, 64), f32)], axis=0)
    weight_parts = split3(weights)

    def combine(k, carry):
        _, inside = sectors(k)
        chunk_weights = []
        for h in range(2):
            hot = hot_ref[pl.ds(pl.multiple_of(k * 128 + h * 64, 64), 64), :]
            chunk_weights.append(sum(dot_nn(part, hot) for part in weight_parts))
        base = pl.multiple_of(k * CH * 64, 64)
        total = jnp.zeros((64, 128), f32)
        for c in range(CH):
            weight = jnp.where(inside, chunk_weights[0][c : c + 1], chunk_weights[1][c : c + 1])
            total = total + weight * map_ref[pl.ds(base + c * 64, 64), :]
        wide = jnp.concatenate([total, total], axis=0).T
        comb_ref[...] = wide
        pair = jnp.where(chunk < 64, comb_ref[pl.ds(0, 64, stride=2), :], comb_ref[pl.ds(1, 64, stride=2), :])
        out_ref[k] = pair
        return carry

    lax.fori_loop(0, NCYC, combine, 0)


def map_call(orders, lens, data):
    stage1, twiddle, stage2 = tables()
    smem, vmem = pl.BlockSpec(memory_space=pltpu.SMEM), pl.BlockSpec(memory_space=pltpu.VMEM)
    return pl.pallas_call(
        map_kernel,
        out_shape=jax.ShapeDtypeStruct((NCYC, 64, 128), f32),
        in_specs=[smem, smem] + [vmem] * 5,
        out_specs=vmem,
        scratch_shapes=[
            pltpu.VMEM((N_DEV * 6, 128), f32),
            pltpu.VMEM((M, 128), f32),
            pltpu.VMEM((NCYC * 2 * CH * NM2, 128), f32),
            pltpu.VMEM((NCYC * CH * 64, 128), f32),
            pltpu.VMEM((CH * 16, 128), f32),
            pltpu.VMEM((CH * 16, 128), f32),
            pltpu.VMEM((NCYC * 128, 128), bf16),
            pltpu.VMEM((CH * 16, 64), f32),
            pltpu.VMEM((128, 128), f32),
            pltpu.VMEM((8, 128), f32),
        ],
        compiler_params=pltpu.CompilerParams(vmem_limit_bytes=40 * 2**20),
    )(orders, lens, data, lens.reshape(1, NCYC * NSEC), stage1, twiddle, stage2)


def per_device(coeffs, legendre, m_order, sector_len):
    first_slot = (lax.axis_index("blk") * N_CHAN + lax.axis_index("chan")) * NSLOT
    orders = lax.dynamic_slice_in_dim(m_order, first_slot, NSLOT, 0)
    parts = jnp.moveaxis(coeffs.reshape(3, 2, N_CHAN, NSLOT, LB), 2, 0)
    parts = lax.all_to_all(parts, "chan", 0, 0, tiled=True)
    sent = legendre_call(orders, parts.reshape(2 * CH, NSLOT, LB), legendre[0])
    data = lax.all_to_all(sent.reshape(N_DEV, 1, ROWS * 128), ("chan", "blk"), 0, 0, tiled=True)
    out = map_call(m_order, sector_len, data.reshape(N_DEV * ROWS, 128))
    return out.reshape(NCYC, PIX)


def solution(mesh):
    placed = (
        P("chan", None, "blk", None),
        P("chan", "blk", None, None),
        P(),
        P(("chan", "blk"), None),
    )
    return jax.shard_map(
        per_device, mesh=mesh, in_specs=placed, out_specs=P(("chan", "blk"), None), check_vma=False
    )
```

profile of v0, /device:TPU:1, one launch (start us, length us, event | category | flops | bytes accessed | tf_op | source)
XLA Modules:
  0.0 91.1 jit_solution(11153686603619574295)
XLA Ops:
  0.0 2.9 %copy.14 = bf16[3,2,4,24,1536]{4,3,1,0,2:T(8,128)(2,1)} copy(bf16[3,2,4,24,1536]{4,3,2,1,0:T(8,128)(2,1)} %bitcast.16) | data formatting | bytes 3538944 | tf_op jit(solution)/shard_map/reshape | solution.py:304
  2.9 0.0 copy-start.3
  2.9 5.0 %all-to-all-start = ((bf16[4,3,2,24,1536]{4,3,2,1,0:T(8,128)(2,1)}), bf16[4,3,2,24,1536]{4,3,2,1,0:T(8,128)(2,1)S(1)}, u32[]{:S(2)}, u32[]{:S(2)}) async-start(bf16[4,3,2,24,1536]{4,3,2,1,0:T(8,128)(2,1)} %bitcast.10), calls=%async_computation | async-start | bytes 3538944 | tf_op jit(solution)/shard_map/all_to_all | solution.py:305
  7.9 0.0 copy-done.3
  7.9 0.1 dynamic_slice.3.orders_ref
  8.0 21.8 %all-to-all-done = bf16[4,3,2,24,1536]{4,3,2,1,0:T(8,128)(2,1)S(1)} async-done(((bf16[4,3,2,24,1536]{4,3,2,1,0:T(8,128)(2,1)}), bf16[4,3,2,24,1536]{4,3,2,1,0:T(8,128)(2,1)S(1)}, u32[]{:S(2)}, u32[]{:S(2)}) %all-to-all-start) | async-done | bytes 1769504 | tf_op jit(solution)/shard_map/all_to_all | solution.py:305
  29.8 12.1 %shard_map.73 = f32[2304,128]{1,0:T(8,128)} custom-call(s32[24]{0:T(128)S(1)} %dynamic_slice.3.orders_ref, bf16[24,24,1536]{2,1,0:T(8,128)(2,1)S(1)} %bitcast.12, bf16[24,256,1536]{2,1,0:T(8,128)(2,1)} %bitcast.15), custom_call_target="tpu_custom_call" | custom-call | tf_op jit(solution)/shard_map/pallas_call | solution.py:115
  41.9 0.0 copy-start.4
  41.9 0.0 copy-start
  41.9 0.0 copy-start.1
  41.9 0.0 copy-start.2
  41.9 10.0 %all-to-all-start.1 = ((f32[128,1,2304]{2,1,0:T(1,128)}), f32[128,1,2304]{2,1,0:T(1,128)S(1)}, u32[]{:S(2)}, u32[]{:S(2)}) async-start(f32[128,1,2304]{2,1,0:T(1,128)} %bitcast.4), calls=%async_computation.1 | async-start | bytes 2359296 | tf_op jit(solution)/shard_map/all_to_all | solution.py:307
  51.9 0.0 copy-done.4
  51.9 0.1 reshape.22.lane_len_ref
  52.0 20.4 %all-to-all-done.1 = f32[128,1,2304]{2,1,0:T(1,128)S(1)} async-done(((f32[128,1,2304]{2,1,0:T(1,128)}), f32[128,1,2304]{2,1,0:T(1,128)S(1)}, u32[]{:S(2)}, u32[]{:S(2)}) %all-to-all-start.1) | async-done | bytes 1179680 | tf_op jit(solution)/shard_map/all_to_all | solution.py:307
  72.4 0.0 copy-done
  72.4 0.0 copy-done.1
  72.4 0.0 copy-done.2
  72.4 17.9 %shard_map.74 = f32[4,64,128]{2,1,0:T(8,128)S(1)} custom-call(s32[3072]{0:T(1024)S(1)} %copy-done.3, s32[4,16]{1,0:T(4,128)S(1)} %copy-done.4, f32[2304,128]{1,0:T(8,128)S(1)} %bitcast.13, s32[1,64]{1,0:T(1,128)S(1)} %reshape.22.lane_len_ref, bf16[128,144]{1,0:T(8,128)(2,1)S(1)} %copy-done.1, f32[128,128]{1,0:T(8,128)S(1)} %copy-done.2, ...), custom_call_target="tpu_custom_call" | custom-call | tf_op jit(solution)/shard_map/pallas_call | solution.py:280
  90.4 0.7 copy.15
Async XLA Ops:
  2.9 5.0 %copy-start.3 = (s32[3072]{0:T(1024)S(1)}, s32[3072]{0:T(1024)}, u32[]{:S(2)}) copy-start(s32[3072]{0:T(1024)} %orders_ref.1) | copy-start | bytes 36868
  2.9 26.9 %all-to-all-start = ((bf16[4,3,2,24,1536]{4,3,2,1,0:T(8,128)(2,1)}), bf16[4,3,2,24,1536]{4,3,2,1,0:T(8,128)(2,1)S(1)}, u32[]{:S(2)}, u32[]{:S(2)}) async-start(bf16[4,3,2,24,1536]{4,3,2,1,0:T(8,128)(2,1)} %bitcast.10), calls=%async_computation | async-start | bytes 3538944 | tf_op jit(solution)/shard_map/all_to_all | solution.py:305
  41.9 10.0 %copy-start.4 = (s32[4,16]{1,0:T(4,128)S(1)}, s32[4,16]{1,0:T(4,128)}, u32[]{:S(2)}) copy-start(s32[4,16]{1,0:T(4,128)} %lens_ref.1) | copy-start | bytes 772
  41.9 30.5 %copy-start = (bf16[256,256]{1,0:T(8,128)(2,1)S(1)}, bf16[256,256]{1,0:T(8,128)(2,1)}, u32[]{:S(2)}) copy-start(bf16[256,256]{1,0:T(8,128)(2,1)} %constant.25.clone.stage2_ref) | copy-start | bytes 393220
  41.9 30.5 %copy-start.1 = (bf16[128,144]{1,0:T(8,128)(2,1)S(1)}, bf16[128,144]{1,0:T(8,128)(2,1)}, u32[]{:S(2)}) copy-start(bf16[128,144]{1,0:T(8,128)(2,1)} %constant.23.clone.stage1_ref) | copy-start | bytes 110596
  41.9 30.5 %copy-start.2 = (f32[128,128]{1,0:T(8,128)S(1)}, f32[128,128]{1,0:T(8,128)}, u32[]{:S(2)}) copy-start(f32[128,128]{1,0:T(8,128)} %constant.24.clone.twiddle_ref) | copy-start | bytes 196612
  41.9 30.5 %all-to-all-start.1 = ((f32[128,1,2304]{2,1,0:T(1,128)}), f32[128,1,2304]{2,1,0:T(1,128)S(1)}, u32[]{:S(2)}, u32[]{:S(2)}) async-start(f32[128,1,2304]{2,1,0:T(1,128)} %bitcast.4), calls=%async_computation.1 | async-start | bytes 2359296 | tf_op jit(solution)/shard_map/all_to_all | solution.py:307
where the time goes:
time: 91.5 us; the launch traced here: 91.1 us
  waiting for transfers between devices  42.2 us (46%)
  Pallas kernels  30 us (33%)
  starting transfers between devices  15 us (16%)
  local copies, waits for them, and re-layouts  3.83 us (4%)
    all_to_all x1, waiting for transfers between devices, per_device(): parts = lax.all_to_all(parts, 'chan', 0, 0, tiled=True)  21.8 us
    all_to_all x1, waiting for transfers between devices, per_device(): lax.all_to_all(sent.reshape(N_DEV, 1, ROWS * 128), ('chan', 'blk'), 0, 0,...  20.4 us
    pallas_call x1, Pallas kernels, map_call(): pl.pallas_call(map_kernel, out_shape=jax.ShapeDtypeStruct((NCYC, 64, 128)...  17.9 us
    pallas_call x1, Pallas kernels, legendre_call(): pl.pallas_call(legendre_kernel, out_shape=jax.ShapeDtypeStruct((N_DEV * R...  12.1 us
    all_to_all x1, starting transfers between devices, per_device(): lax.all_to_all(sent.reshape(N_DEV, 1, ROWS * 128), ('chan', 'blk'), 0, 0,...  10 us
    all_to_all x1, starting transfers between devices, per_device(): parts = lax.all_to_all(parts, 'chan', 0, 0, tiled=True)  4.97 us
    reshape x1, local copies, waits for them, and re-layouts, per_device(): parts = jnp.moveaxis(coeffs.reshape(3, 2, N_CHAN, NSLOT, LB), 2, 0)  2.9 us
  transfers between devices with their start and end apart: 2, of which 2 were waited for; matrix products, arithmetic and copies ran while one was open for 0% of the time, Pallas kernels for 0%

commit v1 on v0

--- a/solution.py
+++ b/solution.py
@@ -22,7 +22,14 @@
 RIDGE_FACTOR = 0.05
 
 NA, NB, NM1, NM2 = 128, 64, 128, 24
-ROWS = 18
+PAIRS = 6
+ROWS = 10
+
+CHUNKS = (16, 8)
+VMEM_LEG = 16 * 2**20
+FETCHES = 6
+TOP_CODE = 32000.0
+LN2 = float(np.log(2.0))
 
 f32, bf16 = jnp.float32, jnp.bfloat16
 
@@ -70,92 +77,147 @@
     return lax.dot_general(x, y, (((1,), (1,)), ((), ())), preferred_element_type=f32)
 
 
-def legendre_kernel(orders_ref, coef_ref, leg_ref, out_ref, wide_ref, acc_ref):
-    step = pl.program_id(0)
-
-    @pl.when(step == 0)
-    def _():
-        def widen(i, carry):
-            value = coef_ref[i].astype(f32)
+def fetch_kernel(source_ref, out_ref, sems):
+    step = NSLOT // FETCHES
+    copies = [
+        pltpu.make_async_copy(source_ref.at[pl.ds(i * step, step)], out_ref.at[pl.ds(i * step, step)], sems.at[i])
+        for i in range(FETCHES)
+    ]
+    for copy in copies:
+        copy.start()
+    for copy in copies:
+        copy.wait()
+
+
+def fetch_call(legendre):
+    return pl.pallas_call(
+        fetch_kernel,
+        out_shape=jax.ShapeDtypeStruct(legendre.shape, legendre.dtype),
+        in_specs=[pl.BlockSpec(memory_space=pl.ANY)],
+        out_specs=pl.BlockSpec(memory_space=pltpu.VMEM),
+        scratch_shapes=[pltpu.SemaphoreType.DMA((FETCHES,))],
+        compiler_params=pltpu.CompilerParams(vmem_limit_bytes=VMEM_LEG),
+        cost_estimate=pl.CostEstimate(flops=0, bytes_accessed=2 * legendre.size * 2, transcendentals=0),
+    )(legendre)
+
+
+def legendre_kernel(first, count, has_before, orders_ref, *refs):
+    coef_refs, refs = refs[:4], refs[4:]
+    leg_ref, refs = refs[0], refs[1:]
+    before_ref, refs = (refs[0], refs[1:]) if has_before else (None, refs)
+    out_ref, wide_ref, acc_ref = refs
+
+    me = lax.axis_index("chan")
+    own = (lax.axis_index("blk") * N_CHAN + me) * NSLOT + first
+
+    for k in range(4):
+        source = (me - k) & (N_CHAN - 1)
+        for i in range(6):
+            value = coef_refs[k][i].astype(f32)
+            start = pl.multiple_of((source * 6 + i) * count, 8)
             for j in range(LB // 128):
-                wide_ref[j, pl.ds(i * NSLOT, NSLOT), :] = value[:, j * 128 : (j + 1) * 128]
-            return carry
-
-        lax.fori_loop(0, 2 * CH, widen, 0)
+                wide_ref[j, pl.ds(start, count), :] = value[:, j * 128 : (j + 1) * 128]
+    if has_before:
+        out_ref[...] = before_ref[...]
+    else:
+        out_ref[...] = jnp.zeros_like(out_ref)
 
     degree = (M - LB) + lax.broadcasted_iota(jnp.int32, (1, LB), 1)
     lane = lax.broadcasted_iota(jnp.int32, (64, 128), 1)
     half = lane < 64
     even_group = (lane & 32) == 0
     spare = (lane & 31) >= 24
-    north, south = [], []
-    for u in range(4):
-        slot = step * 4 + u
-        m = orders_ref[slot]
-        coef = jnp.concatenate([wide_ref[j, pl.ds(slot, 2 * CH, stride=NSLOT), :] for j in range(LB // 128)], axis=1)
-        keep = (degree >= m).astype(f32)
-        sign = (1 - 2 * ((degree + m) & 1)).astype(f32) * keep
-        none = jnp.zeros((8, LB), f32)
-        up = jnp.concatenate([coef * keep, none], axis=0).astype(bf16)
-        down = jnp.concatenate([coef * sign, none], axis=0).astype(bf16)
-        rhs = jnp.concatenate([up, up, down, down], axis=0)
-        acc_ref[u] = dot_nt(leg_ref[u], rhs)
-        k0, k1, k2, k3 = (acc_ref[u, pl.ds(k, 64, stride=4), :] for k in range(4))
-        first = jnp.where(even_group, k0, k1)
-        second = jnp.where(even_group, k2, k3)
-        north.append(jnp.where(half, first, pltpu.roll(second, 64, 1)))
-        south.append(jnp.where(half, pltpu.roll(first, 64, 1), second))
-    for hemi, part in enumerate((north, south)):
-        for r in range(3):
-            row = jnp.where(spare, pltpu.roll(part[3], 24 - 8 * r, 1), part[r])
-            out_ref[pl.ds(hemi * 64 * ROWS + 3 * step + r, 64, stride=ROWS), :] = row
-
-
-def legendre_call(orders, coef, legendre):
+
+    def octet(step, carry):
+        north, south = [], []
+        for u in range(8):
+            slot = step * 8 + u
+            m = orders_ref[own + slot]
+            coef = jnp.concatenate(
+                [wide_ref[j, pl.ds(slot, 2 * CH, stride=count), :] for j in range(LB // 128)], axis=1
+            )
+            keep = (degree >= m).astype(f32)
+            sign = (1 - 2 * ((degree + m) & 1)).astype(f32) * keep
+            none = jnp.zeros((8, LB), f32)
+            up = jnp.concatenate([coef * keep, none], axis=0).astype(bf16)
+            down = jnp.concatenate([coef * sign, none], axis=0).astype(bf16)
+            rhs = jnp.concatenate([up, up, down, down], axis=0)
+            acc_ref[u] = dot_nt(leg_ref[first + slot], rhs)
+        top = jnp.maximum(jnp.abs(acc_ref[0]), jnp.abs(acc_ref[1]))
+        for u in range(2, 8):
+            top = jnp.maximum(top, jnp.abs(acc_ref[u]))
+        top = jnp.max(jnp.max(top, axis=0, keepdims=True), axis=1, keepdims=True)
+        top = jnp.broadcast_to(jnp.maximum(top, 1e-30), (8, 128))
+        code = jnp.ceil(jnp.log(top) * (8 / LN2))
+        inverse = (TOP_CODE * jnp.exp(code * (-LN2 / 8)))[0:1]
+        for u in range(8):
+            k0, k1, k2, k3 = (acc_ref[u, pl.ds(k, 64, stride=4), :] for k in range(4))
+            upper = jnp.where(even_group, k0, k1)
+            lower = jnp.where(even_group, k2, k3)
+            north.append(jnp.where(half, upper, pltpu.roll(lower, 64, 1)))
+            south.append(jnp.where(half, pltpu.roll(upper, 64, 1), lower))
+        at = first // 8 + step
+        for hemi, part in enumerate((north, south)):
+            base = hemi * 64 * ROWS
+            for r in range(3):
+                words = []
+                for h in (0, 4):
+                    row = jnp.where(spare, pltpu.roll(part[h + 3], 24 - 8 * r, 1), part[h + r])
+                    words.append(jnp.round(row * inverse).astype(jnp.int32))
+                out_ref[pl.ds(base + 3 * at + r, 64, stride=ROWS), :] = (words[0] & 0xFFFF) | (words[1] << 16)
+            scales = out_ref[pl.ds(base + 9, 64, stride=ROWS), :]
+            code_row = jnp.broadcast_to(code[0:1].astype(jnp.int32), (64, 128))
+            out_ref[pl.ds(base + 9, 64, stride=ROWS), :] = jnp.where(lane == at, code_row, scales)
+        return carry
+
+    lax.fori_loop(0, count // 8, octet, 0)
+
+
+def legendre_call(first, count, orders, coefs, legendre, before=None):
+    smem, vmem = pl.BlockSpec(memory_space=pltpu.SMEM), pl.BlockSpec(memory_space=pltpu.VMEM)
+    args = [orders, *coefs, legendre] + ([] if before is None else [before])
     return pl.pallas_call(
-        legendre_kernel,
-        out_shape=jax.ShapeDtypeStruct((N_DEV * ROWS, 128), f32),
-        grid=(NSLOT // 4,),
-        in_specs=[
-            pl.BlockSpec(memory_space=pltpu.SMEM),
-            pl.BlockSpec((2 * CH, NSLOT, LB), lambda i: (0, 0, 0)),
-            pl.BlockSpec((4, 256, LB), lambda i: (i, 0, 0)),
+        functools.partial(legendre_kernel, first, count, before is not None),
+        out_shape=jax.ShapeDtypeStruct((N_DEV * ROWS, 128), jnp.int32),
+        in_specs=[smem] + [vmem] * (len(args) - 1),
+        out_specs=vmem,
+        scratch_shapes=[
+            pltpu.VMEM((LB // 128, 2 * CH * count, 128), f32),
+            pltpu.VMEM((8, 256, 128), f32),
         ],
-        out_specs=pl.BlockSpec((N_DEV * ROWS, 128), lambda i: (0, 0)),
-        scratch_shapes=[
-            pltpu.VMEM((LB // 128, 2 * CH * NSLOT, 128), f32),
-            pltpu.VMEM((4, 256, 128), f32),
-        ],
-        compiler_params=pltpu.CompilerParams(vmem_limit_bytes=40 * 2**20),
-    )(orders, coef, legendre)
+        compiler_params=pltpu.CompilerParams(vmem_limit_bytes=VMEM_LEG),
+        cost_estimate=pl.CostEstimate(flops=count * 256 * LB * 256, bytes_accessed=count * 256 * LB * 2, transcendentals=0),
+    )(*args)
 
 
 def map_kernel(
     orders_ref, lens_ref, data_ref, lane_len_ref, stage1_ref, twiddle_ref, stage2_ref, out_ref,
-    last_ref, place_ref, turned_ref, map_ref, low_ref, high_ref, hot_ref, cov_ref, comb_ref, final_ref,
+    slot_ref, place_ref, turned_ref, map_ref, low_ref, high_ref, hot_ref, cov_ref, comb_ref, final_ref,
 ):
-    lane = lax.broadcasted_iota(jnp.int32, (8, 128), 1)
-    group = (lane & 31) >> 3
-
-    def gather_last(i, carry):
-        rows = [data_ref[pl.ds(i * 192 + r, 64, stride=3), :] for r in range(3)]
-        wide = lax.broadcasted_iota(jnp.int32, (64, 128), 1)
-        which = (wide & 31) >> 3
-        rolled = [pltpu.roll(rows[r], 128 - (24 - 8 * r), 1) for r in range(3)]
-        value = jnp.where(which == 0, rolled[0], jnp.where(which == 1, rolled[1], rolled[2]))
-        last_ref[pl.ds(pl.multiple_of(i * 64, 64), 64), :] = value
-        return carry
-
-    lax.fori_loop(0, 12, gather_last, 0)
+    lane = lax.broadcasted_iota(jnp.int32, (N_DEV, 128), 1)
+    which = (lane & 31) >> 3
+    codes = data_ref[pl.ds(9, N_DEV, stride=ROWS), :].astype(f32)
+    scales = jnp.exp(codes * (LN2 / 8)) * (1.0 / TOP_CODE)
+    for octet in range(3):
+        scale = scales[:, octet : octet + 1]
+        words = [data_ref[pl.ds(3 * octet + r, N_DEV, stride=ROWS), :] for r in range(3)]
+        for h in range(2):
+            rolled = []
+            for r in range(3):
+                code = words[r] >> 16 if h else (words[r] << 16) >> 16
+                value = code.astype(f32) * scale
+                slot = 8 * octet + 4 * h + r
+                slot_ref[slot * N_DEV : (slot + 1) * N_DEV, :] = value
+                rolled.append(pltpu.roll(value, 128 - (24 - 8 * r), 1))
+            slot = 8 * octet + 4 * h + 3
+            value = jnp.where(which == 0, rolled[0], jnp.where(which == 1, rolled[1], rolled[2]))
+            slot_ref[slot * N_DEV : (slot + 1) * N_DEV, :] = value
 
     def place(src, carry):
         base = ((src & (N_BLK - 1)) * N_CHAN + (src >> 5)) * NSLOT
-        for t in range(6):
-            for r in range(3):
-                m = orders_ref[base + 4 * t + r]
-                place_ref[pl.ds(m, 1), :] = data_ref[pl.ds(src * ROWS + 3 * t + r, 1), :]
-            m = orders_ref[base + 4 * t + 3]
-            place_ref[pl.ds(m, 1), :] = last_ref[pl.ds(src * 6 + t, 1), :]
+        for slot in range(NSLOT):
+            m = orders_ref[base + slot]
+            place_ref[pl.ds(m, 1), :] = slot_ref[pl.ds(slot * N_DEV + src, 1), :]
         return carry
 
     lax.fori_loop(0, N_DEV, place, 0)
@@ -169,23 +231,25 @@
     stage1 = stage1_ref[...]
 
     def transform(i, carry):
-        parts = []
-        for j in range(2):
-            high, low = split2(turned_ref[pl.ds(pl.multiple_of(i * 96 + j * 48, 16), 48), :])
-            parts.append(jnp.concatenate([high, low, high], axis=0))
-        inner = dot_nn(stage1, jnp.concatenate(parts, axis=1))
         tc, ts = twiddle_ref[0:64, :], twiddle_ref[64:128, :]
         outer = []
-        for j in range(2):
-            re, im = inner[0:64, j * 128 : (j + 1) * 128], inner[64:128, j * 128 : (j + 1) * 128]
-            outer.append(jnp.concatenate([re * tc - im * ts, re * ts + im * tc], axis=1))
+        for pair in range(PAIRS):
+            parts = []
+            for j in range(2):
+                start = pl.multiple_of((i * PAIRS + pair) * 96 + j * 48, 16)
+                high, low = split2(turned_ref[pl.ds(start, 48), :])
+                parts.append(jnp.concatenate([high, low, high], axis=0))
+            inner = dot_nn(stage1, jnp.concatenate(parts, axis=1))
+            for j in range(2):
+                re, im = inner[0:64, j * 128 : (j + 1) * 128], inner[64:128, j * 128 : (j + 1) * 128]
+                outer.append(jnp.concatenate([re * tc - im * ts, re * ts + im * tc], axis=1))
         high, low = split2(jnp.concatenate(outer, axis=0))
         both = dot_nn(high, stage2_ref[...])
         maps = both[:, 0:128] + (both[:, 128:256] + dot_nn(low, stage2_ref[:, 0:128]))
-        map_ref[pl.ds(pl.multiple_of(i * 128, 128), 128), :] = maps
+        map_ref[pl.ds(pl.multiple_of(i * PAIRS * 128, 128), PAIRS * 128), :] = maps
         return carry
 
-    lax.fori_loop(0, NCYC * CH // 2, transform, 0)
+    lax.fori_loop(0, NCYC * CH // (2 * PAIRS), transform, 0, unroll=4)
 
     chunk = lax.broadcasted_iota(jnp.int32, (64, 128), 1)
     offset = lax.broadcasted_iota(jnp.int32, (64, 128), 0)
@@ -283,7 +347,7 @@
         in_specs=[smem, smem] + [vmem] * 5,
         out_specs=vmem,
         scratch_shapes=[
-            pltpu.VMEM((N_DEV * 6, 128), f32),
+            pltpu.VMEM((NSLOT * N_DEV, 128), f32),
             pltpu.VMEM((M, 128), f32),
             pltpu.VMEM((NCYC * 2 * CH * NM2, 128), f32),
             pltpu.VMEM((NCYC * CH * 64, 128), f32),
@@ -298,12 +362,27 @@
     )(orders, lens, data, lens.reshape(1, NCYC * NSEC), stage1, twiddle, stage2)
 
 
+def exchange(coeffs, first, count, me):
+    part = coeffs.reshape(6, N_CHAN, NSLOT, LB)[:, :, first : first + count]
+    pieces = {}
+    for k in (0, 2, 1, 3):
+        piece = lax.dynamic_index_in_dim(part, (me + k) & (N_CHAN - 1), 1, keepdims=False)
+        if k:
+            piece = lax.ppermute(piece, "chan", [(i, (i + k) % N_CHAN) for i in range(N_CHAN)])
+        pieces[k] = piece
+    return [pieces[k] for k in range(N_CHAN)]
+
+
 def per_device(coeffs, legendre, m_order, sector_len):
-    first_slot = (lax.axis_index("blk") * N_CHAN + lax.axis_index("chan")) * NSLOT
-    orders = lax.dynamic_slice_in_dim(m_order, first_slot, NSLOT, 0)
-    parts = jnp.moveaxis(coeffs.reshape(3, 2, N_CHAN, NSLOT, LB), 2, 0)
-    parts = lax.all_to_all(parts, "chan", 0, 0, tiled=True)
-    sent = legendre_call(orders, parts.reshape(2 * CH, NSLOT, LB), legendre[0])
+    me = lax.axis_index("chan")
+    sent, first = None, 0
+    pieces = []
+    for count in CHUNKS:
+        pieces.append((first, count, exchange(coeffs, first, count, me)))
+        first += count
+    legendre = fetch_call(legendre[0])
+    for first, count, piece in pieces:
+        sent = legendre_call(first, count, m_order, piece, legendre, sent)
     data = lax.all_to_all(sent.reshape(N_DEV, 1, ROWS * 128), ("chan", "blk"), 0, 0, tiled=True)
     out = map_call(m_order, sector_len, data.reshape(N_DEV * ROWS, 128))
     return out.reshape(NCYC, PIX)

time: 91.5 us -> 67.2 us (0.73)
  waiting for transfers between devices: 42.2 us -> 15.8 us
  Pallas kernels: 30 us -> 21.1 us
  local copies, waits for them, and re-layouts: 3.83 us -> 9.81 us
  starting transfers between devices: 15 us -> 20.1 us
    all_to_all x1 -> x0, waiting for transfers between devices: 21.8 us -> none  [per_device(): parts = lax.all_to_all(parts, 'chan', 0, 0, tiled=True)]
    ppermute x0 -> x6, starting transfers between devices: none -> 8.65 us  [exchange(): lax.ppermute(piece, 'chan', [(i, (i + k) % N_CHAN) for i in range(N_CHAN)])]
    pallas_call x1, Pallas kernels: 17.9 us -> 11 us  [map_call(): pl.pallas_call(map_kernel, out_shape=jax.ShapeDtypeStruct((NCYC, 64, 128)...]
    unnamed x11 -> x13, local copies, waits for them, and re-layouts: 0.77 us -> 7.14 us
    all_to_all x1, waiting for transfers between devices: 20.4 us -> 14.8 us  [per_device(): lax.all_to_all(sent.reshape(N_DEV, 1, ROWS * 128), ('chan', 'blk'), 0, 0,...]
    all_to_all x1 -> x0, starting transfers between devices: 4.97 us -> none  [per_device(): parts = lax.all_to_all(parts, 'chan', 0, 0, tiled=True)]
    reshape x1 -> x0, local copies, waits for them, and re-layouts: 2.9 us -> none  [per_device(): parts = jnp.moveaxis(coeffs.reshape(3, 2, N_CHAN, NSLOT, LB), 2, 0)]
    slice x0 -> x2, local copies, waits for them, and re-layouts: none -> 2.45 us  [exchange(): part = coeffs.reshape(6, N_CHAN, NSLOT, LB)[:, :, first:first + count]]
  transfers between devices with their start and end apart: 2 -> 7, of which waited for: 2 -> 3; matrix products, arithmetic and copies ran while one was open for 0% -> 2% of each run, Pallas kernels for 0% -> 10%
where the time goes in v1:
time: 67.2 us; the launch traced here: 66.9 us
  Pallas kernels  21.1 us (31%)
  starting transfers between devices  20.1 us (30%)
  waiting for transfers between devices  15.8 us (24%)
  local copies, waits for them, and re-layouts  9.81 us (15%)
    all_to_all x1, waiting for transfers between devices, per_device(): lax.all_to_all(sent.reshape(N_DEV, 1, ROWS * 128), ('chan', 'blk'), 0, 0,...  14.8 us
    all_to_all x1, starting transfers between devices, per_device(): lax.all_to_all(sent.reshape(N_DEV, 1, ROWS * 128), ('chan', 'blk'), 0, 0,...  11.4 us
    pallas_call x1, Pallas kernels, map_call(): pl.pallas_call(map_kernel, out_shape=jax.ShapeDtypeStruct((NCYC, 64, 128)...  11 us
    pallas_call x2, Pallas kernels, legendre_call(): pl.pallas_call(functools.partial(legendre_kernel, first, count, before is...  8.81 us
    ppermute x6, starting transfers between devices, exchange(): lax.ppermute(piece, 'chan', [(i, (i + k) % N_CHAN) for i in range(N_CHAN)])  8.65 us
    unnamed x13, local copies, waits for them, and re-layouts  7.14 us
    slice x2, local copies, waits for them, and re-layouts, exchange(): part = coeffs.reshape(6, N_CHAN, NSLOT, LB)[:, :, first:first + count]  2.45 us
  transfers between devices with their start and end apart: 7, of which 3 were waited for; matrix products, arithmetic and copies ran while one was open for 2% of the time, Pallas kernels for 10%

profile of v1, /device:TPU:1, one launch (start us, length us, event | category | flops | bytes accessed | tf_op | source)
XLA Modules:
  0.0 66.9 jit_solution(10666098706984699058)
XLA Ops:
  0.0 1.3 %slice.9 = bf16[6,4,16,1536]{3,2,1,0:T(8,128)(2,1)S(1)} slice(bf16[6,4,24,1536]{3,2,1,0:T(8,128)(2,1)} %bitcast.43), slice={[0:6], [0:4], [0:16], [0:1536]} | slice | bytes 2359296 | tf_op jit(solution)/shard_map/slice | solution.py:366
  1.4 0.1 dynamic-slice_bitcast_fusion
  1.4 2.1 %collective-permute-start.3 = (bf16[6,16,1536]{2,1,0:T(8,128)(2,1)S(1)}, bf16[6,16,1536]{2,1,0:T(8,128)(2,1)S(1)}, u32[]{:S(2)}, u32[]{:S(2)}) collective-permute-start(bf16[6,16,1536]{2,1,0:T(8,128)(2,1)S(1)} %get-tuple-element.7), channel_id=1, source_target_pairs={{0,32},{32,64},{64,96},{96,0},{1,33},{33,65},{65,97},{97,1},{2,34}... | collective-permute-start | bytes 884744 | tf_op jit(solution)/shard_map/ppermute | solution.py:371
  3.6 2.5 %collective-permute-start.4 = (bf16[6,16,1536]{2,1,0:T(8,128)(2,1)S(1)}, bf16[6,16,1536]{2,1,0:T(8,128)(2,1)S(1)}, u32[]{:S(2)}, u32[]{:S(2)}) collective-permute-start(bf16[6,16,1536]{2,1,0:T(8,128)(2,1)S(1)} %get-tuple-element.6), channel_id=1, source_target_pairs={{0,64},{32,96},{64,0},{96,32},{1,65},{33,97},{65,1},{97,33},{2,66}... | collective-permute-start | bytes 884744 | tf_op jit(solution)/shard_map/ppermute | solution.py:371
  6.0 1.2 %collective-permute-start.5 = (bf16[6,16,1536]{2,1,0:T(8,128)(2,1)S(1)}, bf16[6,16,1536]{2,1,0:T(8,128)(2,1)S(1)}, u32[]{:S(2)}, u32[]{:S(2)}) collective-permute-start(bf16[6,16,1536]{2,1,0:T(8,128)(2,1)S(1)} %get-tuple-element.5), channel_id=1, source_target_pairs={{0,96},{32,0},{64,32},{96,64},{1,97},{33,1},{65,33},{97,65},{2,98}... | collective-permute-start | bytes 884744 | tf_op jit(solution)/shard_map/ppermute | solution.py:371
  7.2 1.1 %slice.8 = bf16[6,4,8,1536]{3,2,1,0:T(8,128)(2,1)S(1)} slice(bf16[6,4,24,1536]{3,2,1,0:T(8,128)(2,1)} %bitcast.44), slice={[0:6], [0:4], [16:24], [0:1536]} | slice | bytes 1179648 | tf_op jit(solution)/shard_map/slice | solution.py:366
  8.3 0.1 dynamic-slice_bitcast_fusion.4
  8.3 0.4 collective-permute-start
  8.7 0.9 %collective-permute-start.1 = (bf16[6,8,1536]{2,1,0:T(8,128)(2,1)S(1)}, bf16[6,8,1536]{2,1,0:T(8,128)(2,1)S(1)}, u32[]{:S(2)}, u32[]{:S(2)}) collective-permute-start(bf16[6,8,1536]{2,1,0:T(8,128)(2,1)S(1)} %get-tuple-element.10), channel_id=1, source_target_pairs={{0,64},{32,96},{64,0},{96,32},{1,65},{33,97},{65,1},{97,33},{2,66}... | collective-permute-start | bytes 442376 | tf_op jit(solution)/shard_map/ppermute | solution.py:371
  9.6 6.4 %copy-done = bf16[1,24,256,1536]{3,2,1,0:T(8,128)(2,1)S(1)} copy-done((bf16[1,24,256,1536]{3,2,1,0:T(8,128)(2,1)S(1)}, bf16[1,24,256,1536]{3,2,1,0:T(8,128)(2,1)}, u32[]{:S(2)}) %copy-start) | copy-done | bytes 18874392
  16.0 0.0 copy-start.2
  16.0 1.3 %shard_map.73.refs_4_ = bf16[24,256,1536]{2,1,0:T(8,128)(2,1)S(1)} custom-call(bf16[24,256,1536]{2,1,0:T(8,128)(2,1)S(1)} %bitcast.40), custom_call_target="tpu_custom_call" | custom-call | bytes 37748736 | tf_op jit(solution)/shard_map/pallas_call | solution.py:93
  17.3 0.0 collective-permute-done.3.refs_1_
  17.3 1.7 %collective-permute-start.2 = (bf16[6,8,1536]{2,1,0:T(8,128)(2,1)S(1)}, bf16[6,8,1536]{2,1,0:T(8,128)(2,1)S(1)}, u32[]{:S(2)}, u32[]{:S(2)}) collective-permute-start(bf16[6,8,1536]{2,1,0:T(8,128)(2,1)S(1)} %get-tuple-element.9), channel_id=1, source_target_pairs={{0,96},{32,0},{64,32},{96,64},{1,97},{33,1},{65,33},{97,65},{2,98}... | collective-permute-start | bytes 442376 | tf_op jit(solution)/shard_map/ppermute | solution.py:371
  19.0 0.0 collective-permute-done.4.refs_2_
  19.0 0.2 collective-permute-done.5.refs_3_
  19.1 0.0 copy-done.2
  19.1 5.1 %shard_map.74.refs_5_ = s32[1280,128]{1,0:T(8,128)S(1)} custom-call(s32[3072]{0:T(1024)S(1)} %copy-done.2, bf16[6,16,1536]{2,1,0:T(8,128)(2,1)S(1)} %get-tuple-element.8.refs_0_, bf16[6,16,1536]{2,1,0:T(8,128)(2,1)S(1)} %collective-permute-done.3.refs_1_, bf16[6,16,1536]{2,1,0:T(8,128)(2,1)S(1)} %collective-permute-done.4.refs_2_, ...), custom_call_target="tpu_custom_call" | custom-call | flops 1610612736 | bytes 12582912 | tf_op jit(solution)/shard_map/pallas_call | solution.py:179
  24.3 0.0 collective-permute-done.refs_1_
  24.3 0.8 %collective-permute-done.1.refs_2_ = bf16[6,8,1536]{2,1,0:T(8,128)(2,1)S(1)} collective-permute-done((bf16[6,8,1536]{2,1,0:T(8,128)(2,1)S(1)}, bf16[6,8,1536]{2,1,0:T(8,128)(2,1)S(1)}, u32[]{:S(2)}, u32[]{:S(2)}) %collective-permute-start.1) | collective-permute-done | bytes 147488 | tf_op jit(solution)/shard_map/ppermute | solution.py:371
  25.1 0.0 collective-permute-done.2.refs_3_
  25.1 0.0 copy-start.4
  25.1 3.7 %shard_map.75 = s32[1280,128]{1,0:T(8,128)} custom-call(s32[3072]{0:T(1024)S(1)} %copy-done.2, bf16[6,8,1536]{2,1,0:T(8,128)(2,1)S(1)} %get-tuple-element.12.refs_0_, bf16[6,8,1536]{2,1,0:T(8,128)(2,1)S(1)} %collective-permute-done.refs_1_, bf16[6,8,1536]{2,1,0:T(8,128)(2,1)S(1)} %collective-permute-done.1.refs_2_, ...), custom_call_target="tpu_custom_call" | custom-call | flops 805306368 | bytes 6291456 | tf_op jit(solution)/shard_map/pallas_call | solution.py:179
  28.8 11.4 %all-to-all-start = ((s32[128,1,1280]{2,1,0:T(1,128)}), s32[128,1,1280]{2,1,0:T(1,128)S(1)}, u32[]{:S(2)}, u32[]{:S(2)}) async-start(s32[128,1,1280]{2,1,0:T(1,128)} %bitcast.10), calls=%async_computation | async-start | bytes 1310720 | tf_op jit(solution)/shard_map/all_to_all | solution.py:386
  40.2 0.0 copy-done.5
  40.3 0.1 reshape.19.lane_len_ref
  40.3 14.8 %all-to-all-done = s32[128,1,1280]{2,1,0:T(1,128)S(1)} async-done(((s32[128,1,1280]{2,1,0:T(1,128)}), s32[128,1,1280]{2,1,0:T(1,128)S(1)}, u32[]{:S(2)}, u32[]{:S(2)}) %all-to-all-start) | async-done | bytes 655392 | tf_op jit(solution)/shard_map/all_to_all | solution.py:386
  55.1 0.0 copy-done.1
  55.1 0.0 copy-done.3
  55.1 0.0 copy-done.4
  55.2 11.0 %shard_map.76 = f32[4,64,128]{2,1,0:T(8,128)S(1)} custom-call(s32[3072]{0:T(1024)S(1)} %copy-done.2, s32[4,16]{1,0:T(4,128)S(1)} %copy-done.5, s32[1280,128]{1,0:T(8,128)S(1)} %bitcast.41, s32[1,64]{1,0:T(1,128)S(1)} %reshape.19.lane_len_ref, bf16[128,144]{1,0:T(8,128)(2,1)S(1)} %copy-done.3, f32[128,128]{1,0:T(8,128)S(1)} %copy-done.4, ...), custom_call_target="tpu_custom_call" | custom-call | tf_op jit(solution)/shard_map/pallas_call | solution.py:344
  66.2 0.7 %copy.25 = f32[1,4,64,128]{3,1,2,0:T(4,128)} copy(f32[1,4,64,128]{3,2,1,0:T(8,128)S(1)} %bitcast.42) | data formatting | bytes 262144
  (4 shorter events, 0.0 us)
Async XLA Ops:
  1.4 15.8 %collective-permute-start.3 = (bf16[6,16,1536]{2,1,0:T(8,128)(2,1)S(1)}, bf16[6,16,1536]{2,1,0:T(8,128)(2,1)S(1)}, u32[]{:S(2)}, u32[]{:S(2)}) collective-permute-start(bf16[6,16,1536]{2,1,0:T(8,128)(2,1)S(1)} %get-tuple-element.7), channel_id=1, source_target_pairs={{0,32},{32,64},{64,96},{96,0},{1,33},{33,65},{65,97},{97,1},{2,34}... | collective-permute-start | bytes 884744 | tf_op jit(solution)/shard_map/ppermute | solution.py:371
  3.6 15.4 %collective-permute-start.4 = (bf16[6,16,1536]{2,1,0:T(8,128)(2,1)S(1)}, bf16[6,16,1536]{2,1,0:T(8,128)(2,1)S(1)}, u32[]{:S(2)}, u32[]{:S(2)}) collective-permute-start(bf16[6,16,1536]{2,1,0:T(8,128)(2,1)S(1)} %get-tuple-element.6), channel_id=1, source_target_pairs={{0,64},{32,96},{64,0},{96,32},{1,65},{33,97},{65,1},{97,33},{2,66}... | collective-permute-start | bytes 884744 | tf_op jit(solution)/shard_map/ppermute | solution.py:371
  6.0 13.1 %collective-permute-start.5 = (bf16[6,16,1536]{2,1,0:T(8,128)(2,1)S(1)}, bf16[6,16,1536]{2,1,0:T(8,128)(2,1)S(1)}, u32[]{:S(2)}, u32[]{:S(2)}) collective-permute-start(bf16[6,16,1536]{2,1,0:T(8,128)(2,1)S(1)} %get-tuple-element.5), channel_id=1, source_target_pairs={{0,96},{32,0},{64,32},{96,64},{1,97},{33,1},{65,33},{97,65},{2,98}... | collective-permute-start | bytes 884744 | tf_op jit(solution)/shard_map/ppermute | solution.py:371
  8.3 15.9 %collective-permute-start = (bf16[6,8,1536]{2,1,0:T(8,128)(2,1)S(1)}, bf16[6,8,1536]{2,1,0:T(8,128)(2,1)S(1)}, u32[]{:S(2)}, u32[]{:S(2)}) collective-permute-start(bf16[6,8,1536]{2,1,0:T(8,128)(2,1)S(1)} %get-tuple-element.11), channel_id=1, source_target_pairs={{0,32},{32,64},{64,96},{96,0},{1,33},{33,65},{65,97},{97,1},{2,34}... | collective-permute-start | bytes 442376 | tf_op jit(solution)/shard_map/ppermute | solution.py:371
  8.7 16.4 %collective-permute-start.1 = (bf16[6,8,1536]{2,1,0:T(8,128)(2,1)S(1)}, bf16[6,8,1536]{2,1,0:T(8,128)(2,1)S(1)}, u32[]{:S(2)}, u32[]{:S(2)}) collective-permute-start(bf16[6,8,1536]{2,1,0:T(8,128)(2,1)S(1)} %get-tuple-element.10), channel_id=1, source_target_pairs={{0,64},{32,96},{64,0},{96,32},{1,65},{33,97},{65,1},{97,33},{2,66}... | collective-permute-start | bytes 442376 | tf_op jit(solution)/shard_map/ppermute | solution.py:371
  9.6 6.4 %copy-start = (bf16[1,24,256,1536]{3,2,1,0:T(8,128)(2,1)S(1)}, bf16[1,24,256,1536]{3,2,1,0:T(8,128)(2,1)}, u32[]{:S(2)}) copy-start(bf16[1,24,256,1536]{3,2,1,0:T(8,128)(2,1)} %param.8) | copy-start | bytes 56623108
  16.0 3.2 %copy-start.2 = (s32[3072]{0:T(1024)S(1)}, s32[3072]{0:T(1024)}, u32[]{:S(2)}) copy-start(s32[3072]{0:T(1024)} %orders_ref.5) | copy-start | bytes 36868
  17.3 7.8 %collective-permute-start.2 = (bf16[6,8,1536]{2,1,0:T(8,128)(2,1)S(1)}, bf16[6,8,1536]{2,1,0:T(8,128)(2,1)S(1)}, u32[]{:S(2)}, u32[]{:S(2)}) collective-permute-start(bf16[6,8,1536]{2,1,0:T(8,128)(2,1)S(1)} %get-tuple-element.9), channel_id=1, source_target_pairs={{0,96},{32,0},{64,32},{96,64},{1,97},{33,1},{65,33},{97,65},{2,98}... | collective-permute-start | bytes 442376 | tf_op jit(solution)/shard_map/ppermute | solution.py:371
  25.1 15.1 %copy-start.5 = (s32[4,16]{1,0:T(4,128)S(1)}, s32[4,16]{1,0:T(4,128)}, u32[]{:S(2)}) copy-start(s32[4,16]{1,0:T(4,128)} %lens_ref.1) | copy-start | bytes 772
  25.1 30.0 %copy-start.1 = (bf16[256,256]{1,0:T(8,128)(2,1)S(1)}, bf16[256,256]{1,0:T(8,128)(2,1)}, u32[]{:S(2)}) copy-start(bf16[256,256]{1,0:T(8,128)(2,1)} %constant.42.clone.stage2_ref) | copy-start | bytes 393220
  25.1 30.0 %copy-start.3 = (bf16[128,144]{1,0:T(8,128)(2,1)S(1)}, bf16[128,144]{1,0:T(8,128)(2,1)}, u32[]{:S(2)}) copy-start(bf16[128,144]{1,0:T(8,128)(2,1)} %constant.40.clone.stage1_ref) | copy-start | bytes 110596
  25.1 30.0 %copy-start.4 = (f32[128,128]{1,0:T(8,128)S(1)}, f32[128,128]{1,0:T(8,128)}, u32[]{:S(2)}) copy-start(f32[128,128]{1,0:T(8,128)} %constant.41.clone.twiddle_ref) | copy-start | bytes 196612
  28.8 26.3 %all-to-all-start = ((s32[128,1,1280]{2,1,0:T(1,128)}), s32[128,1,1280]{2,1,0:T(1,128)S(1)}, u32[]{:S(2)}, u32[]{:S(2)}) async-start(s32[128,1,1280]{2,1,0:T(1,128)} %bitcast.10), calls=%async_computation | async-start | bytes 1310720 | tf_op jit(solution)/shard_map/all_to_all | solution.py:386

commit v2 on v1

--- a/solution.py
+++ b/solution.py
@@ -28,6 +28,7 @@
 CHUNKS = (16, 8)
 VMEM_LEG = 16 * 2**20
 FETCHES = 6
+MOMENTS_UNROLL = 4
 TOP_CODE = 32000.0
 LN2 = float(np.log(2.0))
 
@@ -129,9 +130,12 @@
     spare = (lane & 31) >= 24
 
     def octet(step, carry):
-        north, south = [], []
-        for u in range(8):
-            slot = step * 8 + u
+        slots = []
+        for pair in range(4):
+            slot = step * 8 + pair * 2
+            swap = (orders_ref[own + slot] >= M // 2).astype(jnp.int32)
+            slots += [slot + swap, slot + 1 - swap]
+        for u, slot in enumerate(slots):
             m = orders_ref[own + slot]
             coef = jnp.concatenate(
                 [wide_ref[j, pl.ds(slot, 2 * CH, stride=count), :] for j in range(LB // 128)], axis=1
@@ -150,23 +154,24 @@
         top = jnp.broadcast_to(jnp.maximum(top, 1e-30), (8, 128))
         code = jnp.ceil(jnp.log(top) * (8 / LN2))
         inverse = (TOP_CODE * jnp.exp(code * (-LN2 / 8)))[0:1]
-        for u in range(8):
-            k0, k1, k2, k3 = (acc_ref[u, pl.ds(k, 64, stride=4), :] for k in range(4))
-            upper = jnp.where(even_group, k0, k1)
-            lower = jnp.where(even_group, k2, k3)
-            north.append(jnp.where(half, upper, pltpu.roll(lower, 64, 1)))
-            south.append(jnp.where(half, pltpu.roll(upper, 64, 1), lower))
+        north, south = [], []
+        for pair in range(4):
+            words = []
+            for u in (2 * pair, 2 * pair + 1):
+                k0, k1, k2, k3 = (acc_ref[u, pl.ds(k, 64, stride=4), :] for k in range(4))
+                upper = jnp.round(jnp.where(even_group, k0, k1) * inverse).astype(jnp.int32)
+                lower = jnp.round(jnp.where(even_group, k2, k3) * inverse).astype(jnp.int32)
+                words.append((upper & 0xFFFF) | (lower << 16))
+            north.append(jnp.where(half, words[0], pltpu.roll(words[1], 64, 1)))
+            south.append(jnp.where(half, pltpu.roll(words[0], 64, 1), words[1]))
         at = first // 8 + step
+        code_row = jnp.broadcast_to(code[0:1].astype(jnp.int32), (64, 128))
         for hemi, part in enumerate((north, south)):
             base = hemi * 64 * ROWS
             for r in range(3):
-                words = []
-                for h in (0, 4):
-                    row = jnp.where(spare, pltpu.roll(part[h + 3], 24 - 8 * r, 1), part[h + r])
-                    words.append(jnp.round(row * inverse).astype(jnp.int32))
-                out_ref[pl.ds(base + 3 * at + r, 64, stride=ROWS), :] = (words[0] & 0xFFFF) | (words[1] << 16)
+                row = jnp.where(spare, pltpu.roll(part[3], 24 - 8 * r, 1), part[r])
+                out_ref[pl.ds(base + 3 * at + r, 64, stride=ROWS), :] = row
             scales = out_ref[pl.ds(base + 9, 64, stride=ROWS), :]
-            code_row = jnp.broadcast_to(code[0:1].astype(jnp.int32), (64, 128))
             out_ref[pl.ds(base + 9, 64, stride=ROWS), :] = jnp.where(lane == at, code_row, scales)
         return carry
 
@@ -192,41 +197,42 @@
 
 def map_kernel(
     orders_ref, lens_ref, data_ref, lane_len_ref, stage1_ref, twiddle_ref, stage2_ref, out_ref,
-    slot_ref, place_ref, turned_ref, map_ref, low_ref, high_ref, hot_ref, cov_ref, comb_ref, final_ref,
+    pair_ref, place_ref, turned_ref, map_ref, part_ref, sums_ref, bound_ref, hot_ref, cov_ref, spread_ref, comb_ref, final_ref,
 ):
     lane = lax.broadcasted_iota(jnp.int32, (N_DEV, 128), 1)
     which = (lane & 31) >> 3
-    codes = data_ref[pl.ds(9, N_DEV, stride=ROWS), :].astype(f32)
-    scales = jnp.exp(codes * (LN2 / 8)) * (1.0 / TOP_CODE)
+    scales = data_ref[pl.ds(9, N_DEV, stride=ROWS), :]
     for octet in range(3):
-        scale = scales[:, octet : octet + 1]
+        scale = jnp.broadcast_to(scales[:, octet : octet + 1], (N_DEV, 128))
         words = [data_ref[pl.ds(3 * octet + r, N_DEV, stride=ROWS), :] for r in range(3)]
-        for h in range(2):
-            rolled = []
-            for r in range(3):
-                code = words[r] >> 16 if h else (words[r] << 16) >> 16
-                value = code.astype(f32) * scale
-                slot = 8 * octet + 4 * h + r
-                slot_ref[slot * N_DEV : (slot + 1) * N_DEV, :] = value
-                rolled.append(pltpu.roll(value, 128 - (24 - 8 * r), 1))
-            slot = 8 * octet + 4 * h + 3
-            value = jnp.where(which == 0, rolled[0], jnp.where(which == 1, rolled[1], rolled[2]))
-            slot_ref[slot * N_DEV : (slot + 1) * N_DEV, :] = value
+        rolled = [pltpu.roll(words[r], 128 - (24 - 8 * r), 1) for r in range(3)]
+        words.append(jnp.where(which == 0, rolled[0], jnp.where(which == 1, rolled[1], rolled[2])))
+        for r in range(4):
+            pair = 4 * octet + r
+            pair_ref[pair * N_DEV : (pair + 1) * N_DEV, :] = jnp.where(which == 3, scale, words[r])
 
     def place(src, carry):
         base = ((src & (N_BLK - 1)) * N_CHAN + (src >> 5)) * NSLOT
-        for slot in range(NSLOT):
-            m = orders_ref[base + slot]
-            place_ref[pl.ds(m, 1), :] = slot_ref[pl.ds(slot * N_DEV + src, 1), :]
+        for pair in range(NSLOT // 2):
+            m = orders_ref[base + 2 * pair]
+            row = pair_ref[pl.ds(pair * N_DEV + src, 1), :]
+            place_ref[pl.ds(m, 1), :] = row
+            place_ref[pl.ds(M - 1 - m, 1), :] = row
         return carry
 
-    lax.fori_loop(0, N_DEV, place, 0)
-    place_ref[0:1, :] = place_ref[0:1, :] * 0.5
+    lax.fori_loop(0, N_DEV, place, 0, unroll=2)
 
     for m2 in range(NM2):
         block = place_ref[m2 * 128 : (m2 + 1) * 128, :].T
-        for k in range(NCYC):
-            turned_ref[pl.ds(k * 2 * CH * NM2 + m2, 2 * CH, stride=NM2), :] = block[k * 32 : k * 32 + 24]
+        side = 64 * (m2 // (NM2 // 2))
+        scale = jnp.exp(block[side + 24 : side + 25].astype(f32) * (LN2 / 8)) * (1.0 / TOP_CODE)
+        if m2 == 0:
+            scale = jnp.where(lax.broadcasted_iota(jnp.int32, (1, 128), 1) == 0, 0.5 * scale, scale)
+        for k in range(2):
+            word = block[side + k * 32 : side + k * 32 + 24]
+            for h, code in enumerate(((word << 16) >> 16, word >> 16)):
+                start = (k + 2 * h) * 2 * CH * NM2 + m2
+                turned_ref[pl.ds(start, 2 * CH, stride=NM2), :] = code.astype(f32) * scale
 
     stage1 = stage1_ref[...]
 
@@ -253,30 +259,26 @@
 
     chunk = lax.broadcasted_iota(jnp.int32, (64, 128), 1)
     offset = lax.broadcasted_iota(jnp.int32, (64, 128), 0)
-    low_ref[...] = jnp.zeros_like(low_ref)
-    high_ref[...] = jnp.zeros_like(high_ref)
-    cov_ref[...] = jnp.zeros_like(cov_ref)
-
-    def sectors(k):
-        start = chunk * 64
-        which = jnp.zeros((64, 128), jnp.int32)
-        bound = jnp.full((64, 128), PIX, jnp.int32)
+    part_ref[...] = jnp.zeros_like(part_ref)
+
+    hot_row = lax.broadcasted_iota(jnp.int32, (64, 128), 0)
+    for k in range(NCYC):
+        start = lax.broadcasted_iota(jnp.int32, (8, 128), 1) * 64
+        which = jnp.zeros((8, 128), jnp.int32)
+        bound = jnp.full((8, 128), PIX, jnp.int32)
         end = jnp.int32(0)
         for q in range(NSEC):
             end = end + lens_ref[k, q]
             passed = end <= start
             which = which + passed.astype(jnp.int32)
             bound = jnp.minimum(bound, jnp.where(passed, PIX, end))
-        return which, start + offset < bound
+        bound_ref[k * 8 : k * 8 + 8, :] = bound - start
+        for h in range(2):
+            hot = ((hot_row >> 4) == k) & ((hot_row & 15) == which[0:1] + h)
+            hot_ref[:, (k * 2 + h) * 128 : (k * 2 + h + 1) * 128] = hot.astype(bf16)
 
     def moments(k, carry):
-        which, inside = sectors(k)
-        row = lax.broadcasted_iota(jnp.int32, (64, 128), 0)
-        own = (row >> 4) == k
-        hot_low = (own & ((row & 15) == which)).astype(bf16)
-        hot_high = (own & ((row & 15) == which + 1)).astype(bf16)
-        hot_ref[pl.ds(pl.multiple_of(k * 128, 128), 64), :] = hot_low
-        hot_ref[pl.ds(pl.multiple_of(k * 128 + 64, 64), 64), :] = hot_high
+        inside = offset < bound_ref[pl.ds(pl.multiple_of(k * 8, 8), 1), :]
         base = pl.multiple_of(k * CH * 64, 64)
         for i in range(CH):
             value = map_ref[pl.ds(base + i * 64, 64), :]
@@ -284,19 +286,30 @@
             high = jnp.where(inside, 0.0, value)
             for j in range(i, CH):
                 other = map_ref[pl.ds(base + j * 64, 64), :]
-                for part, ref in ((low, low_ref), (high, high_ref)):
-                    total = jnp.sum(part * other, axis=0, keepdims=True)
-                    ref[i * 16 + j : i * 16 + j + 1, :] = total
-                    if i != j:
-                        ref[j * 16 + i : j * 16 + i + 1, :] = total
-        total = cov_ref[...]
-        for ref, hot in ((low_ref, hot_low), (high_ref, hot_high)):
-            for part in split3(ref[...]):
-                total = total + dot_nt(part, hot)
-        cov_ref[...] = total
+                for h, part in enumerate((low, high)):
+                    product = part * other
+                    pairs = [product[b * 16 : b * 16 + 8] + product[b * 16 + 8 : b * 16 + 16] for b in range(4)]
+                    at = (h * CH + i) * 128 + j * 8
+                    part_ref[at : at + 8, :] = (pairs[0] + pairs[1]) + (pairs[2] + pairs[3])
+        for h in range(2):
+            for i in range(CH):
+                at = (h * CH + i) * 128
+                summed = [part_ref[pl.ds(at + b, 16, stride=8), :] for b in range(8)]
+                while len(summed) > 1:
+                    summed = [summed[b] + summed[b + 1] for b in range(0, len(summed), 2)]
+                sums_ref[pl.ds(pl.multiple_of((k * 2 + h) * CH * 16, 16) + i * 16, 16), :] = summed[0]
         return carry
 
-    lax.fori_loop(0, NCYC, moments, 0)
+    lax.fori_loop(0, NCYC, moments, 0, unroll=MOMENTS_UNROLL)
+    sums = jnp.concatenate([sums_ref[g * CH * 16 : (g + 1) * CH * 16, :] for g in range(2 * NCYC)], axis=1)
+    total = None
+    for part in split3(sums):
+        product = dot_nt(part, hot_ref[...])
+        total = product if total is None else total + product
+    cov_ref[...] = total
+    for i in range(CH):
+        for j in range(i + 1, CH):
+            cov_ref[j * 16 + i : j * 16 + i + 1, :] = cov_ref[i * 16 + j : i * 16 + j + 1, :]
 
     scale = 1.0 / lane_len_ref[...].astype(f32)
     sub = lax.broadcasted_iota(jnp.int32, (16, 64), 0)
@@ -316,26 +329,28 @@
     for i in range(1, CH):
         norm = norm + solved[i]
     weights = jnp.concatenate([s / norm for s in solved] + [jnp.zeros((4, 64), f32)], axis=0)
-    weight_parts = split3(weights)
+    spread = dot_nn(jnp.concatenate(split3(weights), axis=0), hot_ref[...])
+    spread = spread[0:16] + (spread[16:32] + spread[32:48])
+    for g in range(2 * NCYC):
+        spread_ref[g * 16 : (g + 1) * 16, :] = spread[:, g * 128 : (g + 1) * 128]
 
     def combine(k, carry):
-        _, inside = sectors(k)
-        chunk_weights = []
-        for h in range(2):
-            hot = hot_ref[pl.ds(pl.multiple_of(k * 128 + h * 64, 64), 64), :]
-            chunk_weights.append(sum(dot_nn(part, hot) for part in weight_parts))
+        inside = offset < bound_ref[pl.ds(pl.multiple_of(k * 8, 8), 1), :]
+        chunk_weights = [spread_ref[pl.ds(pl.multiple_of((k * 2 + h) * 16, 16), 16), :] for h in range(2)]
         base = pl.multiple_of(k * CH * 64, 64)
         total = jnp.zeros((64, 128), f32)
         for c in range(CH):
             weight = jnp.where(inside, chunk_weights[0][c : c + 1], chunk_weights[1][c : c + 1])
             total = total + weight * map_ref[pl.ds(base + c * 64, 64), :]
         wide = jnp.concatenate([total, total], axis=0).T
-        comb_ref[...] = wide
-        pair = jnp.where(chunk < 64, comb_ref[pl.ds(0, 64, stride=2), :], comb_ref[pl.ds(1, 64, stride=2), :])
-        out_ref[k] = pair
+        comb_ref[k] = wide
+        pair = jnp.where(chunk < 64, comb_ref[k, pl.ds(0, 64, stride=2), :], comb_ref[k, pl.ds(1, 64, stride=2), :])
+        final_ref[pl.ds(k, 64, stride=NCYC), :] = pair
         return carry
 
-    lax.fori_loop(0, NCYC, combine, 0)
+    lax.fori_loop(0, NCYC, combine, 0, unroll=4)
+    for i in range(64):
+        out_ref[:, i * 128 : (i + 1) * 128] = final_ref[i * NCYC : (i + 1) * NCYC, :]
 
 
 def map_call(orders, lens, data):
@@ -343,49 +358,69 @@
     smem, vmem = pl.BlockSpec(memory_space=pltpu.SMEM), pl.BlockSpec(memory_space=pltpu.VMEM)
     return pl.pallas_call(
         map_kernel,
-        out_shape=jax.ShapeDtypeStruct((NCYC, 64, 128), f32),
+        out_shape=jax.ShapeDtypeStruct((NCYC, PIX), f32),
         in_specs=[smem, smem] + [vmem] * 5,
         out_specs=vmem,
         scratch_shapes=[
-            pltpu.VMEM((NSLOT * N_DEV, 128), f32),
-            pltpu.VMEM((M, 128), f32),
+            pltpu.VMEM((NSLOT // 2 * N_DEV, 128), jnp.int32),
+            pltpu.VMEM((M, 128), jnp.int32),
             pltpu.VMEM((NCYC * 2 * CH * NM2, 128), f32),
             pltpu.VMEM((NCYC * CH * 64, 128), f32),
-            pltpu.VMEM((CH * 16, 128), f32),
-            pltpu.VMEM((CH * 16, 128), f32),
-            pltpu.VMEM((NCYC * 128, 128), bf16),
+            pltpu.VMEM((2 * CH * 128, 128), f32),
+            pltpu.VMEM((2 * NCYC * CH * 16, 128), f32),
+            pltpu.VMEM((NCYC * 8, 128), jnp.int32),
+            pltpu.VMEM((64, 2 * NCYC * 128), bf16),
             pltpu.VMEM((CH * 16, 64), f32),
-            pltpu.VMEM((128, 128), f32),
-            pltpu.VMEM((8, 128), f32),
+            pltpu.VMEM((2 * NCYC * 16, 128), f32),
+            pltpu.VMEM((NCYC, 128, 128), f32),
+            pltpu.VMEM((64 * NCYC, 128), f32),
         ],
         compiler_params=pltpu.CompilerParams(vmem_limit_bytes=40 * 2**20),
     )(orders, lens, data, lens.reshape(1, NCYC * NSEC), stage1, twiddle, stage2)
 
 
-def exchange(coeffs, first, count, me):
-    part = coeffs.reshape(6, N_CHAN, NSLOT, LB)[:, :, first : first + count]
-    pieces = {}
-    for k in (0, 2, 1, 3):
-        piece = lax.dynamic_index_in_dim(part, (me + k) & (N_CHAN - 1), 1, keepdims=False)
-        if k:
-            piece = lax.ppermute(piece, "chan", [(i, (i + k) % N_CHAN) for i in range(N_CHAN)])
-        pieces[k] = piece
-    return [pieces[k] for k in range(N_CHAN)]
+def slices_kernel(coef_ref, *refs):
+    outs, sems = refs[:-1], refs[-1]
+    me = lax.axis_index("chan")
+    copies, first = [], 0
+    for n, count in enumerate(CHUNKS):
+        for k in (2, 1, 3, 0):
+            source = coef_ref.at[:, (me + k) & (N_CHAN - 1), pl.ds(first, count)]
+            copies.append(pltpu.make_async_copy(source, outs[n * N_CHAN + k], sems.at[n * N_CHAN + k]))
+        first += count
+    for copy in copies:
+        copy.start()
+    for copy in copies:
+        copy.wait()
+
+
+def exchange(coeffs):
+    shapes = [jax.ShapeDtypeStruct((6, count, LB), bf16) for count in CHUNKS for _ in range(N_CHAN)]
+    pieces = pl.pallas_call(
+        slices_kernel,
+        out_shape=shapes,
+        in_specs=[pl.BlockSpec(memory_space=pl.ANY)],
+        out_specs=[pl.BlockSpec(memory_space=pltpu.VMEM)] * len(shapes),
+        scratch_shapes=[pltpu.SemaphoreType.DMA((len(shapes),))],
+        compiler_params=pltpu.CompilerParams(vmem_limit_bytes=VMEM_LEG),
+    )(coeffs.reshape(6, N_CHAN, NSLOT, LB))
+    pieces = list(pieces)
+    for n in range(len(CHUNKS)):
+        for k in (2, 1, 3):
+            at = n * N_CHAN + k
+            pieces[at] = lax.ppermute(pieces[at], "chan", [(i, (i + k) % N_CHAN) for i in range(N_CHAN)])
+    return [pieces[n * N_CHAN : (n + 1) * N_CHAN] for n in range(len(CHUNKS))]
 
 
 def per_device(coeffs, legendre, m_order, sector_len):
-    me = lax.axis_index("chan")
+    pieces = exchange(coeffs)
+    legendre = fetch_call(legendre[0])
     sent, first = None, 0
-    pieces = []
-    for count in CHUNKS:
-        pieces.append((first, count, exchange(coeffs, first, count, me)))
+    for count, piece in zip(CHUNKS, pieces):
+        sent = legendre_call(first, count, m_order, piece, legendre, sent)
         first += count
-    legendre = fetch_call(legendre[0])
-    for first, count, piece in pieces:
-        sent = legendre_call(first, count, m_order, piece, legendre, sent)
     data = lax.all_to_all(sent.reshape(N_DEV, 1, ROWS * 128), ("chan", "blk"), 0, 0, tiled=True)
-    out = map_call(m_order, sector_len, data.reshape(N_DEV * ROWS, 128))
-    return out.reshape(NCYC, PIX)
+    return map_call(m_order, sector_len, data.reshape(N_DEV * ROWS, 128))
 
 
 def solution(mesh):

time: 67.2 us -> 66 us (0.982)
  local copies, waits for them, and re-layouts: 9.81 us -> 7.95 us
  waiting for transfers between devices: 15.8 us -> 16.9 us
    slice x2 -> x0, local copies, waits for them, and re-layouts: 2.45 us -> none  [exchange(): part = coeffs.reshape(6, N_CHAN, NSLOT, LB)[:, :, first:first + count]]
    ppermute x6, waiting for transfers between devices: 0.99 us -> 2.11 us  [exchange(): lax.ppermute(pieces[at], 'chan', [(i, (i + k) % N_CHAN) for i in range(N_...]
    unnamed x13 -> x14, local copies, waits for them, and re-layouts: 7.14 us -> 7.86 us
    pallas_call x1 -> x2, Pallas kernels: 11 us -> 10.3 us  [the longest x1 10 us: map_call(): pl.pallas_call(map_kernel, out_shape=jax.ShapeDtypeStruct((NCYC, PIX), f3...]
  transfers between devices with their start and end apart: 7 -> 7, of which waited for: 3 -> 4; matrix products, arithmetic and copies ran while one was open for 2% -> 0% of each run, Pallas kernels for 10% -> 10%
where the time goes in v2:
time: 66 us; the launch traced here: 65.8 us
  Pallas kernels  20.7 us (31%)
  starting transfers between devices  20.1 us (30%)
  waiting for transfers between devices  16.9 us (26%)
  local copies, waits for them, and re-layouts  7.95 us (12%)
    all_to_all x1, waiting for transfers between devices, per_device(): lax.all_to_all(sent.reshape(N_DEV, 1, ROWS * 128), ('chan', 'blk'), 0, 0,...  14.8 us
    all_to_all x1, starting transfers between devices, per_device(): lax.all_to_all(sent.reshape(N_DEV, 1, ROWS * 128), ('chan', 'blk'), 0, 0,...  11.6 us
    pallas_call x1, Pallas kernels, map_call(): pl.pallas_call(map_kernel, out_shape=jax.ShapeDtypeStruct((NCYC, PIX), f3...  10 us
    pallas_call x2, Pallas kernels, legendre_call(): pl.pallas_call(functools.partial(legendre_kernel, first, count, before is...  9.1 us
    ppermute x6, starting transfers between devices, exchange(): lax.ppermute(pieces[at], 'chan', [(i, (i + k) % N_CHAN) for i in range(N_...  8.49 us
    unnamed x14, local copies, waits for them, and re-layouts  7.86 us
    ppermute x6, waiting for transfers between devices, exchange(): lax.ppermute(pieces[at], 'chan', [(i, (i + k) % N_CHAN) for i in range(N_...  2.11 us
  transfers between devices with their start and end apart: 7, of which 4 were waited for; matrix products, arithmetic and copies ran while one was open for 0% of the time, Pallas kernels for 10%

profile of v2, /device:TPU:1, one launch (start us, length us, event | category | flops | bytes accessed | tf_op | source)
XLA Modules:
  0.0 65.8 jit_solution(875983855962382514)
XLA Ops:
  0.0 0.0 copy-start.1
  0.0 1.5 %copy-done.1 = bf16[3,2,96,1536]{3,2,1,0:T(8,128)(2,1)S(1)} copy-done((bf16[3,2,96,1536]{3,2,1,0:T(8,128)(2,1)S(1)}, bf16[3,2,96,1536]{3,2,1,0:T(8,128)(2,1)}, u32[]{:S(2)}) %copy-start.1) | copy-done | bytes 1769496
  1.5 0.3 shard_map.73
  1.8 2.1 %collective-permute-start.3 = (bf16[6,16,1536]{2,1,0:T(8,128)(2,1)S(1)}, bf16[6,16,1536]{2,1,0:T(8,128)(2,1)S(1)}, u32[]{:S(2)}, u32[]{:S(2)}) collective-permute-start(bf16[6,16,1536]{2,1,0:T(8,128)(2,1)S(1)} %get-tuple-element.18), channel_id=1, source_target_pairs={{0,32},{32,64},{64,96},{96,0},{1,33},{33,65},{65,97},{97,1},{2,34}... | collective-permute-start | bytes 884744 | tf_op jit(solution)/shard_map/ppermute | solution.py:411
  3.9 2.5 %collective-permute-start.4 = (bf16[6,16,1536]{2,1,0:T(8,128)(2,1)S(1)}, bf16[6,16,1536]{2,1,0:T(8,128)(2,1)S(1)}, u32[]{:S(2)}, u32[]{:S(2)}) collective-permute-start(bf16[6,16,1536]{2,1,0:T(8,128)(2,1)S(1)} %get-tuple-element.19), channel_id=1, source_target_pairs={{0,64},{32,96},{64,0},{96,32},{1,65},{33,97},{65,1},{97,33},{2,66}... | collective-permute-start | bytes 884744 | tf_op jit(solution)/shard_map/ppermute | solution.py:411
  6.3 1.2 %collective-permute-start.5 = (bf16[6,16,1536]{2,1,0:T(8,128)(2,1)S(1)}, bf16[6,16,1536]{2,1,0:T(8,128)(2,1)S(1)}, u32[]{:S(2)}, u32[]{:S(2)}) collective-permute-start(bf16[6,16,1536]{2,1,0:T(8,128)(2,1)S(1)} %get-tuple-element.20), channel_id=1, source_target_pairs={{0,96},{32,0},{64,32},{96,64},{1,97},{33,1},{65,33},{97,65},{2,98}... | collective-permute-start | bytes 884744 | tf_op jit(solution)/shard_map/ppermute | solution.py:411
  7.5 0.3 collective-permute-start
  7.8 0.9 %collective-permute-start.1 = (bf16[6,8,1536]{2,1,0:T(8,128)(2,1)S(1)}, bf16[6,8,1536]{2,1,0:T(8,128)(2,1)S(1)}, u32[]{:S(2)}, u32[]{:S(2)}) collective-permute-start(bf16[6,8,1536]{2,1,0:T(8,128)(2,1)S(1)} %get-tuple-element.15), channel_id=1, source_target_pairs={{0,64},{32,96},{64,0},{96,32},{1,65},{33,97},{65,1},{97,33},{2,66}... | collective-permute-start | bytes 442376 | tf_op jit(solution)/shard_map/ppermute | solution.py:411
  8.7 0.0 copy-start
  8.7 6.4 %copy-done = bf16[1,24,256,1536]{3,2,1,0:T(8,128)(2,1)S(1)} copy-done((bf16[1,24,256,1536]{3,2,1,0:T(8,128)(2,1)S(1)}, bf16[1,24,256,1536]{3,2,1,0:T(8,128)(2,1)}, u32[]{:S(2)}) %copy-start) | copy-done | bytes 18874392
  15.0 0.0 copy-start.3
  15.0 1.3 %shard_map.74.refs_4_ = bf16[24,256,1536]{2,1,0:T(8,128)(2,1)S(1)} custom-call(bf16[24,256,1536]{2,1,0:T(8,128)(2,1)S(1)} %bitcast.4), custom_call_target="tpu_custom_call" | custom-call | bytes 37748736 | tf_op jit(solution)/shard_map/pallas_call | solution.py:94
  16.4 0.0 collective-permute-done.3.refs_1_
  16.4 1.6 %collective-permute-start.2 = (bf16[6,8,1536]{2,1,0:T(8,128)(2,1)S(1)}, bf16[6,8,1536]{2,1,0:T(8,128)(2,1)S(1)}, u32[]{:S(2)}, u32[]{:S(2)}) collective-permute-start(bf16[6,8,1536]{2,1,0:T(8,128)(2,1)S(1)} %get-tuple-element.16), channel_id=1, source_target_pairs={{0,96},{32,0},{64,32},{96,64},{1,97},{33,1},{65,33},{97,65},{2,98}... | collective-permute-start | bytes 442376 | tf_op jit(solution)/shard_map/ppermute | solution.py:411
  18.0 1.1 %collective-permute-done.4.refs_2_ = bf16[6,16,1536]{2,1,0:T(8,128)(2,1)S(1)} collective-permute-done((bf16[6,16,1536]{2,1,0:T(8,128)(2,1)S(1)}, bf16[6,16,1536]{2,1,0:T(8,128)(2,1)S(1)}, u32[]{:S(2)}, u32[]{:S(2)}) %collective-permute-start.4) | collective-permute-done | bytes 294944 | tf_op jit(solution)/shard_map/ppermute | solution.py:411
  19.1 0.3 collective-permute-done.5.refs_3_
  19.5 0.0 copy-done.3
  19.5 0.0 copy-start.6
  19.5 0.0 copy-start.5
  19.5 5.3 %shard_map.75.refs_5_ = s32[1280,128]{1,0:T(8,128)S(1)} custom-call(s32[3072]{0:T(1024)S(1)} %copy-done.3, bf16[6,16,1536]{2,1,0:T(8,128)(2,1)S(1)} %get-tuple-element.17.refs_0_, bf16[6,16,1536]{2,1,0:T(8,128)(2,1)S(1)} %collective-permute-done.3.refs_1_, bf16[6,16,1536]{2,1,0:T(8,128)(2,1)S(1)} %collective-permute-done.4.refs_2_, ...), custom_call_target="tpu_custom_call" | custom-call | flops 1610612736 | bytes 12582912 | tf_op jit(solution)/shard_map/pallas_call | solution.py:184
  24.8 0.0 collective-permute-done.refs_1_
  24.8 0.6 collective-permute-done.1.refs_2_
  25.4 0.0 collective-permute-done.2.refs_3_
  25.4 3.8 %shard_map.76 = s32[1280,128]{1,0:T(8,128)} custom-call(s32[3072]{0:T(1024)S(1)} %copy-done.3, bf16[6,8,1536]{2,1,0:T(8,128)(2,1)S(1)} %get-tuple-element.13.refs_0_, bf16[6,8,1536]{2,1,0:T(8,128)(2,1)S(1)} %collective-permute-done.refs_1_, bf16[6,8,1536]{2,1,0:T(8,128)(2,1)S(1)} %collective-permute-done.1.refs_2_, ...), custom_call_target="tpu_custom_call" | custom-call | flops 805306368 | bytes 6291456 | tf_op jit(solution)/shard_map/pallas_call | solution.py:184
  29.2 11.6 %all-to-all-start = ((s32[128,1,1280]{2,1,0:T(1,128)}), s32[128,1,1280]{2,1,0:T(1,128)S(1)}, u32[]{:S(2)}, u32[]{:S(2)}) async-start(s32[128,1,1280]{2,1,0:T(1,128)} %bitcast.2), calls=%async_computation | async-start | bytes 1310720 | tf_op jit(solution)/shard_map/all_to_all | solution.py:422
  40.8 0.0 copy-done.6
  40.9 0.1 reshape.15.lane_len_ref
  40.9 14.8 %all-to-all-done = s32[128,1,1280]{2,1,0:T(1,128)S(1)} async-done(((s32[128,1,1280]{2,1,0:T(1,128)}), s32[128,1,1280]{2,1,0:T(1,128)S(1)}, u32[]{:S(2)}, u32[]{:S(2)}) %all-to-all-start) | async-done | bytes 655392 | tf_op jit(solution)/shard_map/all_to_all | solution.py:422
  55.7 0.0 copy-done.2
  55.7 0.0 copy-done.4
  55.7 0.0 copy-done.5
  55.7 10.0 %shard_map.77 = f32[4,8192]{1,0:T(4,128)} custom-call(s32[3072]{0:T(1024)S(1)} %copy-done.3, s32[4,16]{1,0:T(4,128)S(1)} %copy-done.6, s32[1280,128]{1,0:T(8,128)S(1)} %bitcast.5, s32[1,64]{1,0:T(1,128)S(1)} %reshape.15.lane_len_ref, bf16[128,144]{1,0:T(8,128)(2,1)S(1)} %copy-done.4, f32[128,128]{1,0:T(8,128)S(1)} %copy-done.5, bf16[256,256]{1,0:T(8,128)(2,1)S(1)} %copy-done.2), custom_call_target="tpu_custom_call" | custom-call | tf_op jit(solution)/shard_map/pallas_call | solution.py:359
  (2 shorter events, 0.0 us)
Async XLA Ops:
  0.0 1.5 %copy-start.1 = (bf16[3,2,96,1536]{3,2,1,0:T(8,128)(2,1)S(1)}, bf16[3,2,96,1536]{3,2,1,0:T(8,128)(2,1)}, u32[]{:S(2)}) copy-start(bf16[3,2,96,1536]{3,2,1,0:T(8,128)(2,1)} %param.7) | copy-start | bytes 5308420
  1.8 14.6 %collective-permute-start.3 = (bf16[6,16,1536]{2,1,0:T(8,128)(2,1)S(1)}, bf16[6,16,1536]{2,1,0:T(8,128)(2,1)S(1)}, u32[]{:S(2)}, u32[]{:S(2)}) collective-permute-start(bf16[6,16,1536]{2,1,0:T(8,128)(2,1)S(1)} %get-tuple-element.18), channel_id=1, source_target_pairs={{0,32},{32,64},{64,96},{96,0},{1,33},{33,65},{65,97},{97,1},{2,34}... | collective-permute-start | bytes 884744 | tf_op jit(solution)/shard_map/ppermute | solution.py:411
  3.9 15.2 %collective-permute-start.4 = (bf16[6,16,1536]{2,1,0:T(8,128)(2,1)S(1)}, bf16[6,16,1536]{2,1,0:T(8,128)(2,1)S(1)}, u32[]{:S(2)}, u32[]{:S(2)}) collective-permute-start(bf16[6,16,1536]{2,1,0:T(8,128)(2,1)S(1)} %get-tuple-element.19), channel_id=1, source_target_pairs={{0,64},{32,96},{64,0},{96,32},{1,65},{33,97},{65,1},{97,33},{2,66}... | collective-permute-start | bytes 884744 | tf_op jit(solution)/shard_map/ppermute | solution.py:411
  6.3 13.1 %collective-permute-start.5 = (bf16[6,16,1536]{2,1,0:T(8,128)(2,1)S(1)}, bf16[6,16,1536]{2,1,0:T(8,128)(2,1)S(1)}, u32[]{:S(2)}, u32[]{:S(2)}) collective-permute-start(bf16[6,16,1536]{2,1,0:T(8,128)(2,1)S(1)} %get-tuple-element.20), channel_id=1, source_target_pairs={{0,96},{32,0},{64,32},{96,64},{1,97},{33,1},{65,33},{97,65},{2,98}... | collective-permute-start | bytes 884744 | tf_op jit(solution)/shard_map/ppermute | solution.py:411
  7.5 17.3 %collective-permute-start = (bf16[6,8,1536]{2,1,0:T(8,128)(2,1)S(1)}, bf16[6,8,1536]{2,1,0:T(8,128)(2,1)S(1)}, u32[]{:S(2)}, u32[]{:S(2)}) collective-permute-start(bf16[6,8,1536]{2,1,0:T(8,128)(2,1)S(1)} %get-tuple-element.14), channel_id=1, source_target_pairs={{0,32},{32,64},{64,96},{96,0},{1,33},{33,65},{65,97},{97,1},{2,34}... | collective-permute-start | bytes 442376 | tf_op jit(solution)/shard_map/ppermute | solution.py:411
  7.8 17.6 %collective-permute-start.1 = (bf16[6,8,1536]{2,1,0:T(8,128)(2,1)S(1)}, bf16[6,8,1536]{2,1,0:T(8,128)(2,1)S(1)}, u32[]{:S(2)}, u32[]{:S(2)}) collective-permute-start(bf16[6,8,1536]{2,1,0:T(8,128)(2,1)S(1)} %get-tuple-element.15), channel_id=1, source_target_pairs={{0,64},{32,96},{64,0},{96,32},{1,65},{33,97},{65,1},{97,33},{2,66}... | collective-permute-start | bytes 442376 | tf_op jit(solution)/shard_map/ppermute | solution.py:411
  8.7 6.4 %copy-start = (bf16[1,24,256,1536]{3,2,1,0:T(8,128)(2,1)S(1)}, bf16[1,24,256,1536]{3,2,1,0:T(8,128)(2,1)}, u32[]{:S(2)}) copy-start(bf16[1,24,256,1536]{3,2,1,0:T(8,128)(2,1)} %param.8) | copy-start | bytes 56623108
  15.0 4.4 %copy-start.3 = (s32[3072]{0:T(1024)S(1)}, s32[3072]{0:T(1024)}, u32[]{:S(2)}) copy-start(s32[3072]{0:T(1024)} %orders_ref.5) | copy-start | bytes 36868
  16.4 9.1 %collective-permute-start.2 = (bf16[6,8,1536]{2,1,0:T(8,128)(2,1)S(1)}, bf16[6,8,1536]{2,1,0:T(8,128)(2,1)S(1)}, u32[]{:S(2)}, u32[]{:S(2)}) collective-permute-start(bf16[6,8,1536]{2,1,0:T(8,128)(2,1)S(1)} %get-tuple-element.16), channel_id=1, source_target_pairs={{0,96},{32,0},{64,32},{96,64},{1,97},{33,1},{65,33},{97,65},{2,98}... | collective-permute-start | bytes 442376 | tf_op jit(solution)/shard_map/ppermute | solution.py:411
  19.5 21.4 %copy-start.6 = (s32[4,16]{1,0:T(4,128)S(1)}, s32[4,16]{1,0:T(4,128)}, u32[]{:S(2)}) copy-start(s32[4,16]{1,0:T(4,128)} %lens_ref.1) | copy-start | bytes 772
  19.5 36.3 %copy-start.2 = (bf16[256,256]{1,0:T(8,128)(2,1)S(1)}, bf16[256,256]{1,0:T(8,128)(2,1)}, u32[]{:S(2)}) copy-start(bf16[256,256]{1,0:T(8,128)(2,1)} %constant.8.clone.stage2_ref) | copy-start | bytes 393220
  19.5 36.3 %copy-start.4 = (bf16[128,144]{1,0:T(8,128)(2,1)S(1)}, bf16[128,144]{1,0:T(8,128)(2,1)}, u32[]{:S(2)}) copy-start(bf16[128,144]{1,0:T(8,128)(2,1)} %constant.6.clone.stage1_ref) | copy-start | bytes 110596
  19.5 36.3 %copy-start.5 = (f32[128,128]{1,0:T(8,128)S(1)}, f32[128,128]{1,0:T(8,128)}, u32[]{:S(2)}) copy-start(f32[128,128]{1,0:T(8,128)} %constant.7.clone.twiddle_ref) | copy-start | bytes 196612
  29.2 26.5 %all-to-all-start = ((s32[128,1,1280]{2,1,0:T(1,128)}), s32[128,1,1280]{2,1,0:T(1,128)S(1)}, u32[]{:S(2)}, u32[]{:S(2)}) async-start(s32[128,1,1280]{2,1,0:T(1,128)} %bitcast.2), calls=%async_computation | async-start | bytes 1310720 | tf_op jit(solution)/shard_map/all_to_all | solution.py:422

commit v3 on v2

--- a/solution.py
+++ b/solution.py
@@ -28,6 +28,7 @@
 CHUNKS = (16, 8)
 VMEM_LEG = 16 * 2**20
 FETCHES = 6
+ORDER = (2, 1, 3)
 MOMENTS_UNROLL = 4
 TOP_CODE = 32000.0
 LN2 = float(np.log(2.0))
@@ -130,32 +131,32 @@
     spare = (lane & 31) >= 24
 
     def octet(step, carry):
-        slots = []
+        at = first // 8 + step
+        north, south = [], []
+        code_row = jnp.zeros((8, 128), jnp.int32)
         for pair in range(4):
             slot = step * 8 + pair * 2
             swap = (orders_ref[own + slot] >= M // 2).astype(jnp.int32)
-            slots += [slot + swap, slot + 1 - swap]
-        for u, slot in enumerate(slots):
-            m = orders_ref[own + slot]
-            coef = jnp.concatenate(
-                [wide_ref[j, pl.ds(slot, 2 * CH, stride=count), :] for j in range(LB // 128)], axis=1
-            )
-            keep = (degree >= m).astype(f32)
-            sign = (1 - 2 * ((degree + m) & 1)).astype(f32) * keep
-            none = jnp.zeros((8, LB), f32)
-            up = jnp.concatenate([coef * keep, none], axis=0).astype(bf16)
-            down = jnp.concatenate([coef * sign, none], axis=0).astype(bf16)
-            rhs = jnp.concatenate([up, up, down, down], axis=0)
-            acc_ref[u] = dot_nt(leg_ref[first + slot], rhs)
-        top = jnp.maximum(jnp.abs(acc_ref[0]), jnp.abs(acc_ref[1]))
-        for u in range(2, 8):
-            top = jnp.maximum(top, jnp.abs(acc_ref[u]))
-        top = jnp.max(jnp.max(top, axis=0, keepdims=True), axis=1, keepdims=True)
-        top = jnp.broadcast_to(jnp.maximum(top, 1e-30), (8, 128))
-        code = jnp.ceil(jnp.log(top) * (8 / LN2))
-        inverse = (TOP_CODE * jnp.exp(code * (-LN2 / 8)))[0:1]
-        north, south = [], []
-        for pair in range(4):
+            top = None
+            for u, slot in ((2 * pair, slot + swap), (2 * pair + 1, slot + 1 - swap)):
+                m = orders_ref[own + slot]
+                coef = jnp.concatenate(
+                    [wide_ref[j, pl.ds(slot, 2 * CH, stride=count), :] for j in range(LB // 128)], axis=1
+                )
+                keep = (degree >= m).astype(f32)
+                sign = (1 - 2 * ((degree + m) & 1)).astype(f32) * keep
+                none = jnp.zeros((8, LB), f32)
+                up = jnp.concatenate([coef * keep, none], axis=0).astype(bf16)
+                down = jnp.concatenate([coef * sign, none], axis=0).astype(bf16)
+                rhs = jnp.concatenate([up, up, down, down], axis=0)
+                product = dot_nt(leg_ref[first + slot], rhs)
+                acc_ref[u] = product
+                most = jnp.max(jnp.abs(product), axis=0, keepdims=True)
+                top = most if top is None else jnp.maximum(top, most)
+            top = jnp.max(jnp.broadcast_to(top, (8, 128)), axis=1, keepdims=True)
+            code = jnp.ceil(jnp.log(jnp.broadcast_to(jnp.maximum(top, 1e-30), (8, 128))) * (8 / LN2))
+            inverse = (TOP_CODE * jnp.exp(code * (-LN2 / 8)))[0:1]
+            code_row = jnp.where(lane[0:8] == 4 * at + pair, code.astype(jnp.int32), code_row)
             words = []
             for u in (2 * pair, 2 * pair + 1):
                 k0, k1, k2, k3 = (acc_ref[u, pl.ds(k, 64, stride=4), :] for k in range(4))
@@ -164,18 +165,17 @@
                 words.append((upper & 0xFFFF) | (lower << 16))
             north.append(jnp.where(half, words[0], pltpu.roll(words[1], 64, 1)))
             south.append(jnp.where(half, pltpu.roll(words[0], 64, 1), words[1]))
-        at = first // 8 + step
-        code_row = jnp.broadcast_to(code[0:1].astype(jnp.int32), (64, 128))
+        code_row = jnp.broadcast_to(code_row[0:1], (64, 128))
         for hemi, part in enumerate((north, south)):
             base = hemi * 64 * ROWS
             for r in range(3):
                 row = jnp.where(spare, pltpu.roll(part[3], 24 - 8 * r, 1), part[r])
                 out_ref[pl.ds(base + 3 * at + r, 64, stride=ROWS), :] = row
             scales = out_ref[pl.ds(base + 9, 64, stride=ROWS), :]
-            out_ref[pl.ds(base + 9, 64, stride=ROWS), :] = jnp.where(lane == at, code_row, scales)
+            out_ref[pl.ds(base + 9, 64, stride=ROWS), :] = jnp.where((lane >> 2) == at, code_row, scales)
         return carry
 
-    lax.fori_loop(0, count // 8, octet, 0)
+    lax.fori_loop(0, count // 8, octet, 0, unroll=count // 8)
 
 
 def legendre_call(first, count, orders, coefs, legendre, before=None):
@@ -203,12 +203,12 @@
     which = (lane & 31) >> 3
     scales = data_ref[pl.ds(9, N_DEV, stride=ROWS), :]
     for octet in range(3):
-        scale = jnp.broadcast_to(scales[:, octet : octet + 1], (N_DEV, 128))
         words = [data_ref[pl.ds(3 * octet + r, N_DEV, stride=ROWS), :] for r in range(3)]
         rolled = [pltpu.roll(words[r], 128 - (24 - 8 * r), 1) for r in range(3)]
         words.append(jnp.where(which == 0, rolled[0], jnp.where(which == 1, rolled[1], rolled[2])))
         for r in range(4):
             pair = 4 * octet + r
+            scale = jnp.broadcast_to(scales[:, pair : pair + 1], (N_DEV, 128))
             pair_ref[pair * N_DEV : (pair + 1) * N_DEV, :] = jnp.where(which == 3, scale, words[r])
 
     def place(src, carry):
@@ -394,7 +394,7 @@
         copy.wait()
 
 
-def exchange(coeffs):
+def cut(coeffs):
     shapes = [jax.ShapeDtypeStruct((6, count, LB), bf16) for count in CHUNKS for _ in range(N_CHAN)]
     pieces = pl.pallas_call(
         slices_kernel,
@@ -404,17 +404,21 @@
         scratch_shapes=[pltpu.SemaphoreType.DMA((len(shapes),))],
         compiler_params=pltpu.CompilerParams(vmem_limit_bytes=VMEM_LEG),
     )(coeffs.reshape(6, N_CHAN, NSLOT, LB))
+    return [list(pieces[n * N_CHAN : (n + 1) * N_CHAN]) for n in range(len(CHUNKS))]
+
+
+def send(pieces):
     pieces = list(pieces)
-    for n in range(len(CHUNKS)):
-        for k in (2, 1, 3):
-            at = n * N_CHAN + k
-            pieces[at] = lax.ppermute(pieces[at], "chan", [(i, (i + k) % N_CHAN) for i in range(N_CHAN)])
-    return [pieces[n * N_CHAN : (n + 1) * N_CHAN] for n in range(len(CHUNKS))]
+    for k in ORDER:
+        pieces[k] = lax.ppermute(pieces[k], "chan", [(i, (i + k) % N_CHAN) for i in range(N_CHAN)])
+    return pieces
 
 
 def per_device(coeffs, legendre, m_order, sector_len):
-    pieces = exchange(coeffs)
-    legendre = fetch_call(legendre[0])
+    early, late = cut(coeffs)
+    early = send(early)
+    legendre, late = lax.optimization_barrier((fetch_call(legendre[0]), late))
+    pieces = [early, send(late)]
     sent, first = None, 0
     for count, piece in zip(CHUNKS, pieces):
         sent = legendre_call(first, count, m_order, piece, legendre, sent)

time: 66 us -> 65.6 us (level)
    pallas_call x2, Pallas kernels: 9.1 us -> 8.39 us  [legendre_call(): pl.pallas_call(functools.partial(legendre_kernel, first, count, before is...]
  transfers between devices with their start and end apart: 7 -> 7, of which waited for: 4 -> 3; matrix products, arithmetic and copies ran while one was open for 0% -> 0% of each run, Pallas kernels for 10% -> 9%
where the time goes in v3:
time: 65.6 us; the launch traced here: 65.4 us
  Pallas kernels  20.2 us (31%)
  starting transfers between devices  19.8 us (30%)
  waiting for transfers between devices  17.4 us (27%)
  local copies, waits for them, and re-layouts  7.95 us (12%)
    all_to_all x1, waiting for transfers between devices, per_device(): lax.all_to_all(sent.reshape(N_DEV, 1, ROWS * 128), ('chan', 'blk'), 0, 0,...  14.8 us
    all_to_all x1, starting transfers between devices, per_device(): lax.all_to_all(sent.reshape(N_DEV, 1, ROWS * 128), ('chan', 'blk'), 0, 0,...  11.2 us
    pallas_call x1, Pallas kernels, map_call(): pl.pallas_call(map_kernel, out_shape=jax.ShapeDtypeStruct((NCYC, PIX), f3...  10.2 us
    ppermute x6, starting transfers between devices, send(): lax.ppermute(pieces[k], 'chan', [(i, (i + k) % N_CHAN) for i in range(N_C...  8.58 us
    pallas_call x2, Pallas kernels, legendre_call(): pl.pallas_call(functools.partial(legendre_kernel, first, count, before is...  8.39 us
    unnamed x14, local copies, waits for them, and re-layouts  7.87 us
    ppermute x6, waiting for transfers between devices, send(): lax.ppermute(pieces[k], 'chan', [(i, (i + k) % N_CHAN) for i in range(N_C...  2.62 us
    pallas_call x1, Pallas kernels, fetch_call(): pl.pallas_call(fetch_kernel, out_shape=jax.ShapeDtypeStruct(legendre.shap...  1.32 us
  transfers between devices with their start and end apart: 7, of which 3 were waited for; matrix products, arithmetic and copies ran while one was open for 0% of the time, Pallas kernels for 9%

profile of v3, /device:TPU:1, one launch (start us, length us, event | category | flops | bytes accessed | tf_op | source)
XLA Modules:
  0.0 65.4 jit_solution(10538016396000006692)
XLA Ops:
  0.0 1.5 %copy-done.1 = bf16[3,2,96,1536]{3,2,1,0:T(8,128)(2,1)S(1)} copy-done((bf16[3,2,96,1536]{3,2,1,0:T(8,128)(2,1)S(1)}, bf16[3,2,96,1536]{3,2,1,0:T(8,128)(2,1)}, u32[]{:S(2)}) %copy-start.1) | copy-done | bytes 1769496
  1.5 0.3 shard_map.74
  1.8 2.1 %collective-permute-start.3 = (bf16[6,16,1536]{2,1,0:T(8,128)(2,1)S(1)}, bf16[6,16,1536]{2,1,0:T(8,128)(2,1)S(1)}, u32[]{:S(2)}, u32[]{:S(2)}) collective-permute-start(bf16[6,16,1536]{2,1,0:T(8,128)(2,1)S(1)} %get-tuple-element.28), channel_id=1, source_target_pairs={{0,32},{32,64},{64,96},{96,0},{1,33},{33,65},{65,97},{97,1},{2,34}... | collective-permute-start | bytes 884744 | tf_op jit(solution)/shard_map/ppermute | solution.py:413
  3.9 2.5 %collective-permute-start.4 = (bf16[6,16,1536]{2,1,0:T(8,128)(2,1)S(1)}, bf16[6,16,1536]{2,1,0:T(8,128)(2,1)S(1)}, u32[]{:S(2)}, u32[]{:S(2)}) collective-permute-start(bf16[6,16,1536]{2,1,0:T(8,128)(2,1)S(1)} %get-tuple-element.29), channel_id=1, source_target_pairs={{0,64},{32,96},{64,0},{96,32},{1,65},{33,97},{65,1},{97,33},{2,66}... | collective-permute-start | bytes 884744 | tf_op jit(solution)/shard_map/ppermute | solution.py:413
  6.3 1.2 %collective-permute-start.5 = (bf16[6,16,1536]{2,1,0:T(8,128)(2,1)S(1)}, bf16[6,16,1536]{2,1,0:T(8,128)(2,1)S(1)}, u32[]{:S(2)}, u32[]{:S(2)}) collective-permute-start(bf16[6,16,1536]{2,1,0:T(8,128)(2,1)S(1)} %get-tuple-element.30), channel_id=1, source_target_pairs={{0,96},{32,0},{64,32},{96,64},{1,97},{33,1},{65,33},{97,65},{2,98}... | collective-permute-start | bytes 884744 | tf_op jit(solution)/shard_map/ppermute | solution.py:413
  7.5 0.0 copy-start
  7.5 6.4 %copy-done = bf16[1,24,256,1536]{3,2,1,0:T(8,128)(2,1)S(1)} copy-done((bf16[1,24,256,1536]{3,2,1,0:T(8,128)(2,1)S(1)}, bf16[1,24,256,1536]{3,2,1,0:T(8,128)(2,1)}, u32[]{:S(2)}) %copy-start) | copy-done | bytes 18874392
  13.9 0.0 copy-start.3
  13.9 1.3 %shard_map.73.refs_4_ = bf16[24,256,1536]{2,1,0:T(8,128)(2,1)S(1)} custom-call(bf16[24,256,1536]{2,1,0:T(8,128)(2,1)S(1)} %bitcast.4), custom_call_target="tpu_custom_call" | custom-call | bytes 37748736 | tf_op jit(solution)/shard_map/pallas_call | solution.py:95
  15.2 0.4 collective-permute-start
  15.6 0.9 %collective-permute-start.1 = (bf16[6,8,1536]{2,1,0:T(8,128)(2,1)S(1)}, bf16[6,8,1536]{2,1,0:T(8,128)(2,1)S(1)}, u32[]{:S(2)}, u32[]{:S(2)}) collective-permute-start(bf16[6,8,1536]{2,1,0:T(8,128)(2,1)S(1)} %get-tuple-element.24), channel_id=1, source_target_pairs={{0,64},{32,96},{64,0},{96,32},{1,65},{33,97},{65,1},{97,33},{2,66}... | collective-permute-start | bytes 442376 | tf_op jit(solution)/shard_map/ppermute | solution.py:413
  16.4 0.0 collective-permute-done.3.refs_1_
  16.4 1.6 %collective-permute-start.2 = (bf16[6,8,1536]{2,1,0:T(8,128)(2,1)S(1)}, bf16[6,8,1536]{2,1,0:T(8,128)(2,1)S(1)}, u32[]{:S(2)}, u32[]{:S(2)}) collective-permute-start(bf16[6,8,1536]{2,1,0:T(8,128)(2,1)S(1)} %get-tuple-element.25), channel_id=1, source_target_pairs={{0,96},{32,0},{64,32},{96,64},{1,97},{33,1},{65,33},{97,65},{2,98}... | collective-permute-start | bytes 442376 | tf_op jit(solution)/shard_map/ppermute | solution.py:413
  18.1 1.0 %collective-permute-done.4.refs_2_ = bf16[6,16,1536]{2,1,0:T(8,128)(2,1)S(1)} collective-permute-done((bf16[6,16,1536]{2,1,0:T(8,128)(2,1)S(1)}, bf16[6,16,1536]{2,1,0:T(8,128)(2,1)S(1)}, u32[]{:S(2)}, u32[]{:S(2)}) %collective-permute-start.4) | collective-permute-done | bytes 294944 | tf_op jit(solution)/shard_map/ppermute | solution.py:413
  19.1 0.0 collective-permute-done.5.refs_3_
  19.1 0.0 copy-done.3
  19.1 0.0 copy-start.2
  19.1 0.0 copy-start.4
  19.1 0.0 copy-start.5
  19.1 4.7 %shard_map.75.refs_5_ = s32[1280,128]{1,0:T(8,128)S(1)} custom-call(s32[3072]{0:T(1024)S(1)} %copy-done.3, bf16[6,16,1536]{2,1,0:T(8,128)(2,1)S(1)} %get-tuple-element.27.refs_0_, bf16[6,16,1536]{2,1,0:T(8,128)(2,1)S(1)} %collective-permute-done.3.refs_1_, bf16[6,16,1536]{2,1,0:T(8,128)(2,1)S(1)} %collective-permute-done.4.refs_2_, ...), custom_call_target="tpu_custom_call" | custom-call | flops 1610612736 | bytes 12582912 | tf_op jit(solution)/shard_map/pallas_call | solution.py:184
  23.8 0.0 collective-permute-done.refs_1_
  23.8 1.6 %collective-permute-done.1.refs_2_ = bf16[6,8,1536]{2,1,0:T(8,128)(2,1)S(1)} collective-permute-done((bf16[6,8,1536]{2,1,0:T(8,128)(2,1)S(1)}, bf16[6,8,1536]{2,1,0:T(8,128)(2,1)S(1)}, u32[]{:S(2)}, u32[]{:S(2)}) %collective-permute-start.1) | collective-permute-done | bytes 147488 | tf_op jit(solution)/shard_map/ppermute | solution.py:413
  25.4 0.0 collective-permute-done.2.refs_3_
  25.4 3.7 %shard_map.76 = s32[1280,128]{1,0:T(8,128)} custom-call(s32[3072]{0:T(1024)S(1)} %copy-done.3, bf16[6,8,1536]{2,1,0:T(8,128)(2,1)S(1)} %get-tuple-element.22.refs_0_, bf16[6,8,1536]{2,1,0:T(8,128)(2,1)S(1)} %collective-permute-done.refs_1_, bf16[6,8,1536]{2,1,0:T(8,128)(2,1)S(1)} %collective-permute-done.1.refs_2_, ...), custom_call_target="tpu_custom_call" | custom-call | flops 805306368 | bytes 6291456 | tf_op jit(solution)/shard_map/pallas_call | solution.py:184
  29.1 11.2 %all-to-all-start = ((s32[128,1,1280]{2,1,0:T(1,128)}), s32[128,1,1280]{2,1,0:T(1,128)S(1)}, u32[]{:S(2)}, u32[]{:S(2)}) async-start(s32[128,1,1280]{2,1,0:T(1,128)} %bitcast.2), calls=%async_computation | async-start | bytes 1310720 | tf_op jit(solution)/shard_map/all_to_all | solution.py:426
  40.3 0.0 copy-done.6
  40.3 0.1 reshape.15.lane_len_ref
  40.4 14.8 %all-to-all-done = s32[128,1,1280]{2,1,0:T(1,128)S(1)} async-done(((s32[128,1,1280]{2,1,0:T(1,128)}), s32[128,1,1280]{2,1,0:T(1,128)S(1)}, u32[]{:S(2)}, u32[]{:S(2)}) %all-to-all-start) | async-done | bytes 655392 | tf_op jit(solution)/shard_map/all_to_all | solution.py:426
  55.2 0.0 copy-done.2
  55.2 0.0 copy-done.4
  55.2 0.0 copy-done.5
  55.2 10.2 %shard_map.77 = f32[4,8192]{1,0:T(4,128)} custom-call(s32[3072]{0:T(1024)S(1)} %copy-done.3, s32[4,16]{1,0:T(4,128)S(1)} %copy-done.6, s32[1280,128]{1,0:T(8,128)S(1)} %bitcast.5, s32[1,64]{1,0:T(1,128)S(1)} %reshape.15.lane_len_ref, bf16[128,144]{1,0:T(8,128)(2,1)S(1)} %copy-done.4, f32[128,128]{1,0:T(8,128)S(1)} %copy-done.5, bf16[256,256]{1,0:T(8,128)(2,1)S(1)} %copy-done.2), custom_call_target="tpu_custom_call" | custom-call | tf_op jit(solution)/shard_map/pallas_call | solution.py:359
  (2 shorter events, 0.0 us)
Async XLA Ops:
  0.0 1.5 %copy-start.1 = (bf16[3,2,96,1536]{3,2,1,0:T(8,128)(2,1)S(1)}, bf16[3,2,96,1536]{3,2,1,0:T(8,128)(2,1)}, u32[]{:S(2)}) copy-start(bf16[3,2,96,1536]{3,2,1,0:T(8,128)(2,1)} %param.7) | copy-start | bytes 5308420
  1.8 14.7 %collective-permute-start.3 = (bf16[6,16,1536]{2,1,0:T(8,128)(2,1)S(1)}, bf16[6,16,1536]{2,1,0:T(8,128)(2,1)S(1)}, u32[]{:S(2)}, u32[]{:S(2)}) collective-permute-start(bf16[6,16,1536]{2,1,0:T(8,128)(2,1)S(1)} %get-tuple-element.28), channel_id=1, source_target_pairs={{0,32},{32,64},{64,96},{96,0},{1,33},{33,65},{65,97},{97,1},{2,34}... | collective-permute-start | bytes 884744 | tf_op jit(solution)/shard_map/ppermute | solution.py:413
  3.9 15.2 %collective-permute-start.4 = (bf16[6,16,1536]{2,1,0:T(8,128)(2,1)S(1)}, bf16[6,16,1536]{2,1,0:T(8,128)(2,1)S(1)}, u32[]{:S(2)}, u32[]{:S(2)}) collective-permute-start(bf16[6,16,1536]{2,1,0:T(8,128)(2,1)S(1)} %get-tuple-element.29), channel_id=1, source_target_pairs={{0,64},{32,96},{64,0},{96,32},{1,65},{33,97},{65,1},{97,33},{2,66}... | collective-permute-start | bytes 884744 | tf_op jit(solution)/shard_map/ppermute | solution.py:413
  6.3 12.7 %collective-permute-start.5 = (bf16[6,16,1536]{2,1,0:T(8,128)(2,1)S(1)}, bf16[6,16,1536]{2,1,0:T(8,128)(2,1)S(1)}, u32[]{:S(2)}, u32[]{:S(2)}) collective-permute-start(bf16[6,16,1536]{2,1,0:T(8,128)(2,1)S(1)} %get-tuple-element.30), channel_id=1, source_target_pairs={{0,96},{32,0},{64,32},{96,64},{1,97},{33,1},{65,33},{97,65},{2,98}... | collective-permute-start | bytes 884744 | tf_op jit(solution)/shard_map/ppermute | solution.py:413
  7.5 6.4 %copy-start = (bf16[1,24,256,1536]{3,2,1,0:T(8,128)(2,1)S(1)}, bf16[1,24,256,1536]{3,2,1,0:T(8,128)(2,1)}, u32[]{:S(2)}) copy-start(bf16[1,24,256,1536]{3,2,1,0:T(8,128)(2,1)} %param.8) | copy-start | bytes 56623108
  13.9 5.2 %copy-start.3 = (s32[3072]{0:T(1024)S(1)}, s32[3072]{0:T(1024)}, u32[]{:S(2)}) copy-start(s32[3072]{0:T(1024)} %orders_ref.5) | copy-start | bytes 36868
  15.2 8.6 %collective-permute-start = (bf16[6,8,1536]{2,1,0:T(8,128)(2,1)S(1)}, bf16[6,8,1536]{2,1,0:T(8,128)(2,1)S(1)}, u32[]{:S(2)}, u32[]{:S(2)}) collective-permute-start(bf16[6,8,1536]{2,1,0:T(8,128)(2,1)S(1)} %get-tuple-element.23), channel_id=1, source_target_pairs={{0,32},{32,64},{64,96},{96,0},{1,33},{33,65},{65,97},{97,1},{2,34}... | collective-permute-start | bytes 442376 | tf_op jit(solution)/shard_map/ppermute | solution.py:413
  15.6 9.8 %collective-permute-start.1 = (bf16[6,8,1536]{2,1,0:T(8,128)(2,1)S(1)}, bf16[6,8,1536]{2,1,0:T(8,128)(2,1)S(1)}, u32[]{:S(2)}, u32[]{:S(2)}) collective-permute-start(bf16[6,8,1536]{2,1,0:T(8,128)(2,1)S(1)} %get-tuple-element.24), channel_id=1, source_target_pairs={{0,64},{32,96},{64,0},{96,32},{1,65},{33,97},{65,1},{97,33},{2,66}... | collective-permute-start | bytes 442376 | tf_op jit(solution)/shard_map/ppermute | solution.py:413
  16.4 8.9 %collective-permute-start.2 = (bf16[6,8,1536]{2,1,0:T(8,128)(2,1)S(1)}, bf16[6,8,1536]{2,1,0:T(8,128)(2,1)S(1)}, u32[]{:S(2)}, u32[]{:S(2)}) collective-permute-start(bf16[6,8,1536]{2,1,0:T(8,128)(2,1)S(1)} %get-tuple-element.25), channel_id=1, source_target_pairs={{0,96},{32,0},{64,32},{96,64},{1,97},{33,1},{65,33},{97,65},{2,98}... | collective-permute-start | bytes 442376 | tf_op jit(solution)/shard_map/ppermute | solution.py:413
  19.1 21.2 %copy-start.6 = (s32[4,16]{1,0:T(4,128)S(1)}, s32[4,16]{1,0:T(4,128)}, u32[]{:S(2)}) copy-start(s32[4,16]{1,0:T(4,128)} %lens_ref.1) | copy-start | bytes 772
  19.1 36.1 %copy-start.2 = (bf16[256,256]{1,0:T(8,128)(2,1)S(1)}, bf16[256,256]{1,0:T(8,128)(2,1)}, u32[]{:S(2)}) copy-start(bf16[256,256]{1,0:T(8,128)(2,1)} %constant.8.clone.stage2_ref) | copy-start | bytes 393220
  19.1 36.1 %copy-start.4 = (bf16[128,144]{1,0:T(8,128)(2,1)S(1)}, bf16[128,144]{1,0:T(8,128)(2,1)}, u32[]{:S(2)}) copy-start(bf16[128,144]{1,0:T(8,128)(2,1)} %constant.6.clone.stage1_ref) | copy-start | bytes 110596
  19.1 36.1 %copy-start.5 = (f32[128,128]{1,0:T(8,128)S(1)}, f32[128,128]{1,0:T(8,128)}, u32[]{:S(2)}) copy-start(f32[128,128]{1,0:T(8,128)} %constant.7.clone.twiddle_ref) | copy-start | bytes 196612
  29.1 26.1 %all-to-all-start = ((s32[128,1,1280]{2,1,0:T(1,128)}), s32[128,1,1280]{2,1,0:T(1,128)S(1)}, u32[]{:S(2)}, u32[]{:S(2)}) async-start(s32[128,1,1280]{2,1,0:T(1,128)} %bitcast.2), calls=%async_computation | async-start | bytes 1310720 | tf_op jit(solution)/shard_map/all_to_all | solution.py:426

commit v4 on v3

--- a/solution.py
+++ b/solution.py
@@ -195,9 +195,41 @@
     )(*args)
 
 
+def sector_kernel(lens_ref, bound_ref, hot_ref):
+    hot_row = lax.broadcasted_iota(jnp.int32, (64, 128), 0)
+    for k in range(NCYC):
+        start = lax.broadcasted_iota(jnp.int32, (8, 128), 1) * 64
+        which = jnp.zeros((8, 128), jnp.int32)
+        bound = jnp.full((8, 128), PIX, jnp.int32)
+        end = jnp.int32(0)
+        for q in range(NSEC):
+            end = end + lens_ref[k, q]
+            passed = end <= start
+            which = which + passed.astype(jnp.int32)
+            bound = jnp.minimum(bound, jnp.where(passed, PIX, end))
+        bound_ref[k * 8 : k * 8 + 8, :] = bound - start
+        for h in range(2):
+            hot = ((hot_row >> 4) == k) & ((hot_row & 15) == which[0:1] + h)
+            hot_ref[:, (k * 2 + h) * 128 : (k * 2 + h + 1) * 128] = hot.astype(bf16)
+
+
+def sector_call(lens):
+    vmem = pl.BlockSpec(memory_space=pltpu.VMEM)
+    return pl.pallas_call(
+        sector_kernel,
+        out_shape=[
+            jax.ShapeDtypeStruct((NCYC * 8, 128), jnp.int32),
+            jax.ShapeDtypeStruct((64, 2 * NCYC * 128), bf16),
+        ],
+        in_specs=[pl.BlockSpec(memory_space=pltpu.SMEM)],
+        out_specs=[vmem, vmem],
+        compiler_params=pltpu.CompilerParams(vmem_limit_bytes=VMEM_LEG),
+    )(lens)
+
+
 def map_kernel(
-    orders_ref, lens_ref, data_ref, lane_len_ref, stage1_ref, twiddle_ref, stage2_ref, out_ref,
-    pair_ref, place_ref, turned_ref, map_ref, part_ref, sums_ref, bound_ref, hot_ref, cov_ref, spread_ref, comb_ref, final_ref,
+    orders_ref, data_ref, lane_len_ref, stage1_ref, twiddle_ref, stage2_ref, bound_ref, hot_ref, out_ref,
+    pair_ref, place_ref, turned_ref, map_ref, part_ref, sums_ref, cov_ref, spread_ref, comb_ref, final_ref,
 ):
     lane = lax.broadcasted_iota(jnp.int32, (N_DEV, 128), 1)
     which = (lane & 31) >> 3
@@ -259,24 +291,6 @@
 
     chunk = lax.broadcasted_iota(jnp.int32, (64, 128), 1)
     offset = lax.broadcasted_iota(jnp.int32, (64, 128), 0)
-    part_ref[...] = jnp.zeros_like(part_ref)
-
-    hot_row = lax.broadcasted_iota(jnp.int32, (64, 128), 0)
-    for k in range(NCYC):
-        start = lax.broadcasted_iota(jnp.int32, (8, 128), 1) * 64
-        which = jnp.zeros((8, 128), jnp.int32)
-        bound = jnp.full((8, 128), PIX, jnp.int32)
-        end = jnp.int32(0)
-        for q in range(NSEC):
-            end = end + lens_ref[k, q]
-            passed = end <= start
-            which = which + passed.astype(jnp.int32)
-            bound = jnp.minimum(bound, jnp.where(passed, PIX, end))
-        bound_ref[k * 8 : k * 8 + 8, :] = bound - start
-        for h in range(2):
-            hot = ((hot_row >> 4) == k) & ((hot_row & 15) == which[0:1] + h)
-            hot_ref[:, (k * 2 + h) * 128 : (k * 2 + h + 1) * 128] = hot.astype(bf16)
-
     def moments(k, carry):
         inside = offset < bound_ref[pl.ds(pl.multiple_of(k * 8, 8), 1), :]
         base = pl.multiple_of(k * CH * 64, 64)
@@ -353,13 +367,13 @@
         out_ref[:, i * 128 : (i + 1) * 128] = final_ref[i * NCYC : (i + 1) * NCYC, :]
 
 
-def map_call(orders, lens, data):
+def map_call(orders, lens, data, sectors):
     stage1, twiddle, stage2 = tables()
     smem, vmem = pl.BlockSpec(memory_space=pltpu.SMEM), pl.BlockSpec(memory_space=pltpu.VMEM)
     return pl.pallas_call(
         map_kernel,
         out_shape=jax.ShapeDtypeStruct((NCYC, PIX), f32),
-        in_specs=[smem, smem] + [vmem] * 5,
+        in_specs=[smem] + [vmem] * 7,
         out_specs=vmem,
         scratch_shapes=[
             pltpu.VMEM((NSLOT // 2 * N_DEV, 128), jnp.int32),
@@ -368,15 +382,13 @@
             pltpu.VMEM((NCYC * CH * 64, 128), f32),
             pltpu.VMEM((2 * CH * 128, 128), f32),
             pltpu.VMEM((2 * NCYC * CH * 16, 128), f32),
-            pltpu.VMEM((NCYC * 8, 128), jnp.int32),
-            pltpu.VMEM((64, 2 * NCYC * 128), bf16),
             pltpu.VMEM((CH * 16, 64), f32),
             pltpu.VMEM((2 * NCYC * 16, 128), f32),
             pltpu.VMEM((NCYC, 128, 128), f32),
             pltpu.VMEM((64 * NCYC, 128), f32),
         ],
         compiler_params=pltpu.CompilerParams(vmem_limit_bytes=40 * 2**20),
-    )(orders, lens, data, lens.reshape(1, NCYC * NSEC), stage1, twiddle, stage2)
+    )(orders, data, lens.reshape(1, NCYC * NSEC), stage1, twiddle, stage2, *sectors)
 
 
 def slices_kernel(coef_ref, *refs):
@@ -424,7 +436,7 @@
         sent = legendre_call(first, count, m_order, piece, legendre, sent)
         first += count
     data = lax.all_to_all(sent.reshape(N_DEV, 1, ROWS * 128), ("chan", "blk"), 0, 0, tiled=True)
-    return map_call(m_order, sector_len, data.reshape(N_DEV * ROWS, 128))
+    return map_call(m_order, sector_len, data.reshape(N_DEV * ROWS, 128), sector_call(sector_len))
 
 
 def solution(mesh):

time: 65.6 us -> 65.5 us (level)
  waiting for transfers between devices: 17.4 us -> 16.7 us
    all_to_all x1, waiting for transfers between devices: 14.8 us -> 14.1 us  [per_device(): lax.all_to_all(sent.reshape(N_DEV, 1, ROWS * 128), ('chan', 'blk'), 0, 0,...]
    pallas_call x0 -> x1, Pallas kernels: none -> 0.67 us  [sector_call(): pl.pallas_call(sector_kernel, out_shape=[jax.ShapeDtypeStruct((NCYC * 8,...]
  transfers between devices with their start and end apart: 7 -> 7, of which waited for: 3 -> 3; matrix products, arithmetic and copies ran while one was open for 0% -> 0% of each run, Pallas kernels for 9% -> 10%
where the time goes in v4:
time: 65.5 us; the launch traced here: 65.3 us
  Pallas kernels  20.7 us (32%)
  starting transfers between devices  19.8 us (30%)
  waiting for transfers between devices  16.7 us (25%)
  local copies, waits for them, and re-layouts  7.95 us (12%)
    all_to_all x1, waiting for transfers between devices, per_device(): lax.all_to_all(sent.reshape(N_DEV, 1, ROWS * 128), ('chan', 'blk'), 0, 0,...  14.1 us
    all_to_all x1, starting transfers between devices, per_device(): lax.all_to_all(sent.reshape(N_DEV, 1, ROWS * 128), ('chan', 'blk'), 0, 0,...  11.2 us
    pallas_call x1, Pallas kernels, map_call(): pl.pallas_call(map_kernel, out_shape=jax.ShapeDtypeStruct((NCYC, PIX), f3...  10 us
    ppermute x6, starting transfers between devices, send(): lax.ppermute(pieces[k], 'chan', [(i, (i + k) % N_CHAN) for i in range(N_C...  8.58 us
    pallas_call x2, Pallas kernels, legendre_call(): pl.pallas_call(functools.partial(legendre_kernel, first, count, before is...  8.4 us
    unnamed x14, local copies, waits for them, and re-layouts  7.87 us
    ppermute x6, waiting for transfers between devices, send(): lax.ppermute(pieces[k], 'chan', [(i, (i + k) % N_CHAN) for i in range(N_C...  2.62 us
    pallas_call x1, Pallas kernels, fetch_call(): pl.pallas_call(fetch_kernel, out_shape=jax.ShapeDtypeStruct(legendre.shap...  1.32 us
  transfers between devices with their start and end apart: 7, of which 3 were waited for; matrix products, arithmetic and copies ran while one was open for 0% of the time, Pallas kernels for 10%

profile of v4, /device:TPU:1, one launch (start us, length us, event | category | flops | bytes accessed | tf_op | source)
XLA Modules:
  0.0 65.3 jit_solution(14839111019723817809)
XLA Ops:
  0.0 0.0 copy-start.1
  0.0 1.5 %copy-done.1 = bf16[3,2,96,1536]{3,2,1,0:T(8,128)(2,1)S(1)} copy-done((bf16[3,2,96,1536]{3,2,1,0:T(8,128)(2,1)S(1)}, bf16[3,2,96,1536]{3,2,1,0:T(8,128)(2,1)}, u32[]{:S(2)}) %copy-start.1) | copy-done | bytes 1769496
  1.5 0.3 shard_map.74
  1.8 2.1 %collective-permute-start.3 = (bf16[6,16,1536]{2,1,0:T(8,128)(2,1)S(1)}, bf16[6,16,1536]{2,1,0:T(8,128)(2,1)S(1)}, u32[]{:S(2)}, u32[]{:S(2)}) collective-permute-start(bf16[6,16,1536]{2,1,0:T(8,128)(2,1)S(1)} %get-tuple-element.30), channel_id=1, source_target_pairs={{0,32},{32,64},{64,96},{96,0},{1,33},{33,65},{65,97},{97,1},{2,34}... | collective-permute-start | bytes 884744 | tf_op jit(solution)/shard_map/ppermute | solution.py:425
  3.9 2.5 %collective-permute-start.4 = (bf16[6,16,1536]{2,1,0:T(8,128)(2,1)S(1)}, bf16[6,16,1536]{2,1,0:T(8,128)(2,1)S(1)}, u32[]{:S(2)}, u32[]{:S(2)}) collective-permute-start(bf16[6,16,1536]{2,1,0:T(8,128)(2,1)S(1)} %get-tuple-element.31), channel_id=1, source_target_pairs={{0,64},{32,96},{64,0},{96,32},{1,65},{33,97},{65,1},{97,33},{2,66}... | collective-permute-start | bytes 884744 | tf_op jit(solution)/shard_map/ppermute | solution.py:425
  6.3 1.2 %collective-permute-start.5 = (bf16[6,16,1536]{2,1,0:T(8,128)(2,1)S(1)}, bf16[6,16,1536]{2,1,0:T(8,128)(2,1)S(1)}, u32[]{:S(2)}, u32[]{:S(2)}) collective-permute-start(bf16[6,16,1536]{2,1,0:T(8,128)(2,1)S(1)} %get-tuple-element.32), channel_id=1, source_target_pairs={{0,96},{32,0},{64,32},{96,64},{1,97},{33,1},{65,33},{97,65},{2,98}... | collective-permute-start | bytes 884744 | tf_op jit(solution)/shard_map/ppermute | solution.py:425
  7.5 6.4 %copy-done = bf16[1,24,256,1536]{3,2,1,0:T(8,128)(2,1)S(1)} copy-done((bf16[1,24,256,1536]{3,2,1,0:T(8,128)(2,1)S(1)}, bf16[1,24,256,1536]{3,2,1,0:T(8,128)(2,1)}, u32[]{:S(2)}) %copy-start) | copy-done | bytes 18874392
  13.9 1.3 %shard_map.73.refs_4_ = bf16[24,256,1536]{2,1,0:T(8,128)(2,1)S(1)} custom-call(bf16[24,256,1536]{2,1,0:T(8,128)(2,1)S(1)} %bitcast.4), custom_call_target="tpu_custom_call" | custom-call | bytes 37748736 | tf_op jit(solution)/shard_map/pallas_call | solution.py:95
  15.2 0.4 collective-permute-start
  15.6 0.9 %collective-permute-start.1 = (bf16[6,8,1536]{2,1,0:T(8,128)(2,1)S(1)}, bf16[6,8,1536]{2,1,0:T(8,128)(2,1)S(1)}, u32[]{:S(2)}, u32[]{:S(2)}) collective-permute-start(bf16[6,8,1536]{2,1,0:T(8,128)(2,1)S(1)} %get-tuple-element.26), channel_id=1, source_target_pairs={{0,64},{32,96},{64,0},{96,32},{1,65},{33,97},{65,1},{97,33},{2,66}... | collective-permute-start | bytes 442376 | tf_op jit(solution)/shard_map/ppermute | solution.py:425
  16.4 0.0 collective-permute-done.3.refs_1_
  16.4 1.6 %collective-permute-start.2 = (bf16[6,8,1536]{2,1,0:T(8,128)(2,1)S(1)}, bf16[6,8,1536]{2,1,0:T(8,128)(2,1)S(1)}, u32[]{:S(2)}, u32[]{:S(2)}) collective-permute-start(bf16[6,8,1536]{2,1,0:T(8,128)(2,1)S(1)} %get-tuple-element.27), channel_id=1, source_target_pairs={{0,96},{32,0},{64,32},{96,64},{1,97},{33,1},{65,33},{97,65},{2,98}... | collective-permute-start | bytes 442376 | tf_op jit(solution)/shard_map/ppermute | solution.py:425
  18.1 1.0 %collective-permute-done.4.refs_2_ = bf16[6,16,1536]{2,1,0:T(8,128)(2,1)S(1)} collective-permute-done((bf16[6,16,1536]{2,1,0:T(8,128)(2,1)S(1)}, bf16[6,16,1536]{2,1,0:T(8,128)(2,1)S(1)}, u32[]{:S(2)}, u32[]{:S(2)}) %collective-permute-start.4) | collective-permute-done | bytes 294944 | tf_op jit(solution)/shard_map/ppermute | solution.py:425
  19.1 0.0 collective-permute-done.5.refs_3_
  19.1 0.0 copy-done.3
  19.1 0.0 copy-start.2
  19.1 0.0 copy-start.4
  19.1 0.0 copy-start.5
  19.1 4.7 %shard_map.75.refs_5_ = s32[1280,128]{1,0:T(8,128)S(1)} custom-call(s32[3072]{0:T(1024)S(1)} %copy-done.3, bf16[6,16,1536]{2,1,0:T(8,128)(2,1)S(1)} %get-tuple-element.29.refs_0_, bf16[6,16,1536]{2,1,0:T(8,128)(2,1)S(1)} %collective-permute-done.3.refs_1_, bf16[6,16,1536]{2,1,0:T(8,128)(2,1)S(1)} %collective-permute-done.4.refs_2_, ...), custom_call_target="tpu_custom_call" | custom-call | flops 1610612736 | bytes 12582912 | tf_op jit(solution)/shard_map/pallas_call | solution.py:184
  23.8 0.0 collective-permute-done.refs_1_
  23.8 1.6 %collective-permute-done.1.refs_2_ = bf16[6,8,1536]{2,1,0:T(8,128)(2,1)S(1)} collective-permute-done((bf16[6,8,1536]{2,1,0:T(8,128)(2,1)S(1)}, bf16[6,8,1536]{2,1,0:T(8,128)(2,1)S(1)}, u32[]{:S(2)}, u32[]{:S(2)}) %collective-permute-start.1) | collective-permute-done | bytes 147488 | tf_op jit(solution)/shard_map/ppermute | solution.py:425
  25.4 0.0 collective-permute-done.2.refs_3_
  25.4 3.7 %shard_map.76 = s32[1280,128]{1,0:T(8,128)} custom-call(s32[3072]{0:T(1024)S(1)} %copy-done.3, bf16[6,8,1536]{2,1,0:T(8,128)(2,1)S(1)} %get-tuple-element.24.refs_0_, bf16[6,8,1536]{2,1,0:T(8,128)(2,1)S(1)} %collective-permute-done.refs_1_, bf16[6,8,1536]{2,1,0:T(8,128)(2,1)S(1)} %collective-permute-done.1.refs_2_, ...), custom_call_target="tpu_custom_call" | custom-call | flops 805306368 | bytes 6291456 | tf_op jit(solution)/shard_map/pallas_call | solution.py:184
  29.1 11.2 %all-to-all-start = ((s32[128,1,1280]{2,1,0:T(1,128)}), s32[128,1,1280]{2,1,0:T(1,128)S(1)}, u32[]{:S(2)}, u32[]{:S(2)}) async-start(s32[128,1,1280]{2,1,0:T(1,128)} %bitcast.2), calls=%async_computation | async-start | bytes 1310720 | tf_op jit(solution)/shard_map/all_to_all | solution.py:438
  40.3 0.0 copy-done.6
  40.3 0.1 reshape.15.lane_len_ref
  40.4 0.7 %shard_map.77 = (s32[32,128]{1,0:T(8,128)S(1)}, bf16[64,1024]{1,0:T(8,128)(2,1)S(1)}) custom-call(s32[4,16]{1,0:T(4,128)S(1)} %copy-done.6), custom_call_target="tpu_custom_call" | custom-call | tf_op jit(solution)/shard_map/pallas_call | solution.py:218
  41.1 14.1 %all-to-all-done = s32[128,1,1280]{2,1,0:T(1,128)S(1)} async-done(((s32[128,1,1280]{2,1,0:T(1,128)}), s32[128,1,1280]{2,1,0:T(1,128)S(1)}, u32[]{:S(2)}, u32[]{:S(2)}) %all-to-all-start) | async-done | bytes 655392 | tf_op jit(solution)/shard_map/all_to_all | solution.py:438
  55.2 0.0 copy-done.2
  55.2 0.0 copy-done.4
  55.2 0.0 copy-done.5
  55.2 10.0 %shard_map.78 = f32[4,8192]{1,0:T(4,128)} custom-call(s32[3072]{0:T(1024)S(1)} %copy-done.3, s32[1280,128]{1,0:T(8,128)S(1)} %bitcast.5, s32[1,64]{1,0:T(1,128)S(1)} %reshape.15.lane_len_ref, bf16[128,144]{1,0:T(8,128)(2,1)S(1)} %copy-done.4, f32[128,128]{1,0:T(8,128)S(1)} %copy-done.5, bf16[256,256]{1,0:T(8,128)(2,1)S(1)} %copy-done.2, ...), custom_call_target="tpu_custom_call" | custom-call | tf_op jit(solution)/shard_map/pallas_call | solution.py:373
  (3 shorter events, 0.0 us)
Async XLA Ops:
  0.0 1.5 %copy-start.1 = (bf16[3,2,96,1536]{3,2,1,0:T(8,128)(2,1)S(1)}, bf16[3,2,96,1536]{3,2,1,0:T(8,128)(2,1)}, u32[]{:S(2)}) copy-start(bf16[3,2,96,1536]{3,2,1,0:T(8,128)(2,1)} %param.7) | copy-start | bytes 5308420
  1.8 14.7 %collective-permute-start.3 = (bf16[6,16,1536]{2,1,0:T(8,128)(2,1)S(1)}, bf16[6,16,1536]{2,1,0:T(8,128)(2,1)S(1)}, u32[]{:S(2)}, u32[]{:S(2)}) collective-permute-start(bf16[6,16,1536]{2,1,0:T(8,128)(2,1)S(1)} %get-tuple-element.30), channel_id=1, source_target_pairs={{0,32},{32,64},{64,96},{96,0},{1,33},{33,65},{65,97},{97,1},{2,34}... | collective-permute-start | bytes 884744 | tf_op jit(solution)/shard_map/ppermute | solution.py:425
  3.9 15.2 %collective-permute-start.4 = (bf16[6,16,1536]{2,1,0:T(8,128)(2,1)S(1)}, bf16[6,16,1536]{2,1,0:T(8,128)(2,1)S(1)}, u32[]{:S(2)}, u32[]{:S(2)}) collective-permute-start(bf16[6,16,1536]{2,1,0:T(8,128)(2,1)S(1)} %get-tuple-element.31), channel_id=1, source_target_pairs={{0,64},{32,96},{64,0},{96,32},{1,65},{33,97},{65,1},{97,33},{2,66}... | collective-permute-start | bytes 884744 | tf_op jit(solution)/shard_map/ppermute | solution.py:425
  6.3 12.7 %collective-permute-start.5 = (bf16[6,16,1536]{2,1,0:T(8,128)(2,1)S(1)}, bf16[6,16,1536]{2,1,0:T(8,128)(2,1)S(1)}, u32[]{:S(2)}, u32[]{:S(2)}) collective-permute-start(bf16[6,16,1536]{2,1,0:T(8,128)(2,1)S(1)} %get-tuple-element.32), channel_id=1, source_target_pairs={{0,96},{32,0},{64,32},{96,64},{1,97},{33,1},{65,33},{97,65},{2,98}... | collective-permute-start | bytes 884744 | tf_op jit(solution)/shard_map/ppermute | solution.py:425
  7.5 6.4 %copy-start = (bf16[1,24,256,1536]{3,2,1,0:T(8,128)(2,1)S(1)}, bf16[1,24,256,1536]{3,2,1,0:T(8,128)(2,1)}, u32[]{:S(2)}) copy-start(bf16[1,24,256,1536]{3,2,1,0:T(8,128)(2,1)} %param.8) | copy-start | bytes 56623108
  13.9 5.2 %copy-start.3 = (s32[3072]{0:T(1024)S(1)}, s32[3072]{0:T(1024)}, u32[]{:S(2)}) copy-start(s32[3072]{0:T(1024)} %orders_ref.5) | copy-start | bytes 36868
  15.2 8.6 %collective-permute-start = (bf16[6,8,1536]{2,1,0:T(8,128)(2,1)S(1)}, bf16[6,8,1536]{2,1,0:T(8,128)(2,1)S(1)}, u32[]{:S(2)}, u32[]{:S(2)}) collective-permute-start(bf16[6,8,1536]{2,1,0:T(8,128)(2,1)S(1)} %get-tuple-element.25), channel_id=1, source_target_pairs={{0,32},{32,64},{64,96},{96,0},{1,33},{33,65},{65,97},{97,1},{2,34}... | collective-permute-start | bytes 442376 | tf_op jit(solution)/shard_map/ppermute | solution.py:425
  15.6 9.8 %collective-permute-start.1 = (bf16[6,8,1536]{2,1,0:T(8,128)(2,1)S(1)}, bf16[6,8,1536]{2,1,0:T(8,128)(2,1)S(1)}, u32[]{:S(2)}, u32[]{:S(2)}) collective-permute-start(bf16[6,8,1536]{2,1,0:T(8,128)(2,1)S(1)} %get-tuple-element.26), channel_id=1, source_target_pairs={{0,64},{32,96},{64,0},{96,32},{1,65},{33,97},{65,1},{97,33},{2,66}... | collective-permute-start | bytes 442376 | tf_op jit(solution)/shard_map/ppermute | solution.py:425
  16.4 8.9 %collective-permute-start.2 = (bf16[6,8,1536]{2,1,0:T(8,128)(2,1)S(1)}, bf16[6,8,1536]{2,1,0:T(8,128)(2,1)S(1)}, u32[]{:S(2)}, u32[]{:S(2)}) collective-permute-start(bf16[6,8,1536]{2,1,0:T(8,128)(2,1)S(1)} %get-tuple-element.27), channel_id=1, source_target_pairs={{0,96},{32,0},{64,32},{96,64},{1,97},{33,1},{65,33},{97,65},{2,98}... | collective-permute-start | bytes 442376 | tf_op jit(solution)/shard_map/ppermute | solution.py:425
  19.1 21.2 %copy-start.6 = (s32[4,16]{1,0:T(4,128)S(1)}, s32[4,16]{1,0:T(4,128)}, u32[]{:S(2)}) copy-start(s32[4,16]{1,0:T(4,128)} %lens_ref.1) | copy-start | bytes 772
  19.1 36.1 %copy-start.2 = (bf16[256,256]{1,0:T(8,128)(2,1)S(1)}, bf16[256,256]{1,0:T(8,128)(2,1)}, u32[]{:S(2)}) copy-start(bf16[256,256]{1,0:T(8,128)(2,1)} %constant.8.clone.stage2_ref) | copy-start | bytes 393220
  19.1 36.1 %copy-start.4 = (bf16[128,144]{1,0:T(8,128)(2,1)S(1)}, bf16[128,144]{1,0:T(8,128)(2,1)}, u32[]{:S(2)}) copy-start(bf16[128,144]{1,0:T(8,128)(2,1)} %constant.6.clone.stage1_ref) | copy-start | bytes 110596
  19.1 36.1 %copy-start.5 = (f32[128,128]{1,0:T(8,128)S(1)}, f32[128,128]{1,0:T(8,128)}, u32[]{:S(2)}) copy-start(f32[128,128]{1,0:T(8,128)} %constant.7.clone.twiddle_ref) | copy-start | bytes 196612
  29.1 26.1 %all-to-all-start = ((s32[128,1,1280]{2,1,0:T(1,128)}), s32[128,1,1280]{2,1,0:T(1,128)S(1)}, u32[]{:S(2)}, u32[]{:S(2)}) async-start(s32[128,1,1280]{2,1,0:T(1,128)} %bitcast.2), calls=%async_computation | async-start | bytes 1310720 | tf_op jit(solution)/shard_map/all_to_all | solution.py:438

commit v5 on v4

--- a/solution.py
+++ b/solution.py
@@ -28,7 +28,7 @@
 CHUNKS = (16, 8)
 VMEM_LEG = 16 * 2**20
 FETCHES = 6
-ORDER = (2, 1, 3)
+ORDER = (1, 3, 2)
 MOMENTS_UNROLL = 4
 TOP_CODE = 32000.0
 LN2 = float(np.log(2.0))
@@ -252,7 +252,7 @@
             place_ref[pl.ds(M - 1 - m, 1), :] = row
         return carry
 
-    lax.fori_loop(0, N_DEV, place, 0, unroll=2)
+    lax.fori_loop(0, N_DEV, place, 0, unroll=8)
 
     for m2 in range(NM2):
         block = place_ref[m2 * 128 : (m2 + 1) * 128, :].T

time: 65.5 us -> 65.4 us (level)
  no operation moved by 1% of the time
where the time goes in v5:
time: 65.4 us; the launch traced here: 65.2 us
  Pallas kernels  20.7 us (32%)
  starting transfers between devices  19.8 us (30%)
  waiting for transfers between devices  16.7 us (26%)
  local copies, waits for them, and re-layouts  7.95 us (12%)
    all_to_all x1, waiting for transfers between devices, per_device(): lax.all_to_all(sent.reshape(N_DEV, 1, ROWS * 128), ('chan', 'blk'), 0, 0,...  14.1 us
    all_to_all x1, starting transfers between devices, per_device(): lax.all_to_all(sent.reshape(N_DEV, 1, ROWS * 128), ('chan', 'blk'), 0, 0,...  11.2 us
    pallas_call x1, Pallas kernels, map_call(): pl.pallas_call(map_kernel, out_shape=jax.ShapeDtypeStruct((NCYC, PIX), f3...  10 us
    ppermute x6, starting transfers between devices, send(): lax.ppermute(pieces[k], 'chan', [(i, (i + k) % N_CHAN) for i in range(N_C...  8.58 us
    pallas_call x2, Pallas kernels, legendre_call(): pl.pallas_call(functools.partial(legendre_kernel, first, count, before is...  8.4 us
    unnamed x14, local copies, waits for them, and re-layouts  7.87 us
    ppermute x6, waiting for transfers between devices, send(): lax.ppermute(pieces[k], 'chan', [(i, (i + k) % N_CHAN) for i in range(N_C...  2.62 us
    pallas_call x1, Pallas kernels, fetch_call(): pl.pallas_call(fetch_kernel, out_shape=jax.ShapeDtypeStruct(legendre.shap...  1.32 us
  transfers between devices with their start and end apart: 7, of which 3 were waited for; matrix products, arithmetic and copies ran while one was open for 0% of the time, Pallas kernels for 10%

profile of v5, /device:TPU:1, one launch (start us, length us, event | category | flops | bytes accessed | tf_op | source)
XLA Modules:
  0.0 65.2 jit_solution(12920268600718672461)
XLA Ops:
  0.0 0.0 copy-start.1
  0.0 1.5 %copy-done.1 = bf16[3,2,96,1536]{3,2,1,0:T(8,128)(2,1)S(1)} copy-done((bf16[3,2,96,1536]{3,2,1,0:T(8,128)(2,1)S(1)}, bf16[3,2,96,1536]{3,2,1,0:T(8,128)(2,1)}, u32[]{:S(2)}) %copy-start.1) | copy-done | bytes 1769496
  1.5 0.3 shard_map.74
  1.8 2.1 %collective-permute-start.3 = (bf16[6,16,1536]{2,1,0:T(8,128)(2,1)S(1)}, bf16[6,16,1536]{2,1,0:T(8,128)(2,1)S(1)}, u32[]{:S(2)}, u32[]{:S(2)}) collective-permute-start(bf16[6,16,1536]{2,1,0:T(8,128)(2,1)S(1)} %get-tuple-element.30), channel_id=1, source_target_pairs={{0,32},{32,64},{64,96},{96,0},{1,33},{33,65},{65,97},{97,1},{2,34}... | collective-permute-start | bytes 884744 | tf_op jit(solution)/shard_map/ppermute | solution.py:425
  3.9 2.5 %collective-permute-start.4 = (bf16[6,16,1536]{2,1,0:T(8,128)(2,1)S(1)}, bf16[6,16,1536]{2,1,0:T(8,128)(2,1)S(1)}, u32[]{:S(2)}, u32[]{:S(2)}) collective-permute-start(bf16[6,16,1536]{2,1,0:T(8,128)(2,1)S(1)} %get-tuple-element.31), channel_id=1, source_target_pairs={{0,64},{32,96},{64,0},{96,32},{1,65},{33,97},{65,1},{97,33},{2,66}... | collective-permute-start | bytes 884744 | tf_op jit(solution)/shard_map/ppermute | solution.py:425
  6.3 1.2 %collective-permute-start.5 = (bf16[6,16,1536]{2,1,0:T(8,128)(2,1)S(1)}, bf16[6,16,1536]{2,1,0:T(8,128)(2,1)S(1)}, u32[]{:S(2)}, u32[]{:S(2)}) collective-permute-start(bf16[6,16,1536]{2,1,0:T(8,128)(2,1)S(1)} %get-tuple-element.32), channel_id=1, source_target_pairs={{0,96},{32,0},{64,32},{96,64},{1,97},{33,1},{65,33},{97,65},{2,98}... | collective-permute-start | bytes 884744 | tf_op jit(solution)/shard_map/ppermute | solution.py:425
  7.5 6.4 %copy-done = bf16[1,24,256,1536]{3,2,1,0:T(8,128)(2,1)S(1)} copy-done((bf16[1,24,256,1536]{3,2,1,0:T(8,128)(2,1)S(1)}, bf16[1,24,256,1536]{3,2,1,0:T(8,128)(2,1)}, u32[]{:S(2)}) %copy-start) | copy-done | bytes 18874392
  13.9 1.3 %shard_map.73.refs_4_ = bf16[24,256,1536]{2,1,0:T(8,128)(2,1)S(1)} custom-call(bf16[24,256,1536]{2,1,0:T(8,128)(2,1)S(1)} %bitcast.4), custom_call_target="tpu_custom_call" | custom-call | bytes 37748736 | tf_op jit(solution)/shard_map/pallas_call | solution.py:95
  15.2 0.4 collective-permute-start
  15.6 0.9 %collective-permute-start.1 = (bf16[6,8,1536]{2,1,0:T(8,128)(2,1)S(1)}, bf16[6,8,1536]{2,1,0:T(8,128)(2,1)S(1)}, u32[]{:S(2)}, u32[]{:S(2)}) collective-permute-start(bf16[6,8,1536]{2,1,0:T(8,128)(2,1)S(1)} %get-tuple-element.26), channel_id=1, source_target_pairs={{0,64},{32,96},{64,0},{96,32},{1,65},{33,97},{65,1},{97,33},{2,66}... | collective-permute-start | bytes 442376 | tf_op jit(solution)/shard_map/ppermute | solution.py:425
  16.4 0.0 collective-permute-done.3.refs_1_
  16.4 1.6 %collective-permute-start.2 = (bf16[6,8,1536]{2,1,0:T(8,128)(2,1)S(1)}, bf16[6,8,1536]{2,1,0:T(8,128)(2,1)S(1)}, u32[]{:S(2)}, u32[]{:S(2)}) collective-permute-start(bf16[6,8,1536]{2,1,0:T(8,128)(2,1)S(1)} %get-tuple-element.27), channel_id=1, source_target_pairs={{0,96},{32,0},{64,32},{96,64},{1,97},{33,1},{65,33},{97,65},{2,98}... | collective-permute-start | bytes 442376 | tf_op jit(solution)/shard_map/ppermute | solution.py:425
  18.1 1.0 %collective-permute-done.4.refs_2_ = bf16[6,16,1536]{2,1,0:T(8,128)(2,1)S(1)} collective-permute-done((bf16[6,16,1536]{2,1,0:T(8,128)(2,1)S(1)}, bf16[6,16,1536]{2,1,0:T(8,128)(2,1)S(1)}, u32[]{:S(2)}, u32[]{:S(2)}) %collective-permute-start.4) | collective-permute-done | bytes 294944 | tf_op jit(solution)/shard_map/ppermute | solution.py:425
  19.1 0.0 collective-permute-done.5.refs_3_
  19.1 0.0 copy-done.3
  19.1 0.0 copy-start.2
  19.1 0.0 copy-start.4
  19.1 0.0 copy-start.5
  19.1 4.7 %shard_map.75.refs_5_ = s32[1280,128]{1,0:T(8,128)S(1)} custom-call(s32[3072]{0:T(1024)S(1)} %copy-done.3, bf16[6,16,1536]{2,1,0:T(8,128)(2,1)S(1)} %get-tuple-element.29.refs_0_, bf16[6,16,1536]{2,1,0:T(8,128)(2,1)S(1)} %collective-permute-done.3.refs_1_, bf16[6,16,1536]{2,1,0:T(8,128)(2,1)S(1)} %collective-permute-done.4.refs_2_, ...), custom_call_target="tpu_custom_call" | custom-call | flops 1610612736 | bytes 12582912 | tf_op jit(solution)/shard_map/pallas_call | solution.py:184
  23.8 0.0 collective-permute-done.refs_1_
  23.8 1.6 %collective-permute-done.1.refs_2_ = bf16[6,8,1536]{2,1,0:T(8,128)(2,1)S(1)} collective-permute-done((bf16[6,8,1536]{2,1,0:T(8,128)(2,1)S(1)}, bf16[6,8,1536]{2,1,0:T(8,128)(2,1)S(1)}, u32[]{:S(2)}, u32[]{:S(2)}) %collective-permute-start.1) | collective-permute-done | bytes 147488 | tf_op jit(solution)/shard_map/ppermute | solution.py:425
  25.4 0.0 collective-permute-done.2.refs_3_
  25.4 3.7 %shard_map.76 = s32[1280,128]{1,0:T(8,128)} custom-call(s32[3072]{0:T(1024)S(1)} %copy-done.3, bf16[6,8,1536]{2,1,0:T(8,128)(2,1)S(1)} %get-tuple-element.24.refs_0_, bf16[6,8,1536]{2,1,0:T(8,128)(2,1)S(1)} %collective-permute-done.refs_1_, bf16[6,8,1536]{2,1,0:T(8,128)(2,1)S(1)} %collective-permute-done.1.refs_2_, ...), custom_call_target="tpu_custom_call" | custom-call | flops 805306368 | bytes 6291456 | tf_op jit(solution)/shard_map/pallas_call | solution.py:184
  29.1 11.2 %all-to-all-start = ((s32[128,1,1280]{2,1,0:T(1,128)}), s32[128,1,1280]{2,1,0:T(1,128)S(1)}, u32[]{:S(2)}, u32[]{:S(2)}) async-start(s32[128,1,1280]{2,1,0:T(1,128)} %bitcast.2), calls=%async_computation | async-start | bytes 1310720 | tf_op jit(solution)/shard_map/all_to_all | solution.py:438
  40.3 0.0 copy-done.6
  40.3 0.1 reshape.15.lane_len_ref
  40.4 0.7 %shard_map.77 = (s32[32,128]{1,0:T(8,128)S(1)}, bf16[64,1024]{1,0:T(8,128)(2,1)S(1)}) custom-call(s32[4,16]{1,0:T(4,128)S(1)} %copy-done.6), custom_call_target="tpu_custom_call" | custom-call | tf_op jit(solution)/shard_map/pallas_call | solution.py:218
  41.1 14.1 %all-to-all-done = s32[128,1,1280]{2,1,0:T(1,128)S(1)} async-done(((s32[128,1,1280]{2,1,0:T(1,128)}), s32[128,1,1280]{2,1,0:T(1,128)S(1)}, u32[]{:S(2)}, u32[]{:S(2)}) %all-to-all-start) | async-done | bytes 655392 | tf_op jit(solution)/shard_map/all_to_all | solution.py:438
  55.2 0.0 copy-done.2
  55.2 0.0 copy-done.4
  55.2 0.0 copy-done.5
  55.2 10.0 %shard_map.78 = f32[4,8192]{1,0:T(4,128)} custom-call(s32[3072]{0:T(1024)S(1)} %copy-done.3, s32[1280,128]{1,0:T(8,128)S(1)} %bitcast.5, s32[1,64]{1,0:T(1,128)S(1)} %reshape.15.lane_len_ref, bf16[128,144]{1,0:T(8,128)(2,1)S(1)} %copy-done.4, f32[128,128]{1,0:T(8,128)S(1)} %copy-done.5, bf16[256,256]{1,0:T(8,128)(2,1)S(1)} %copy-done.2, ...), custom_call_target="tpu_custom_call" | custom-call | tf_op jit(solution)/shard_map/pallas_call | solution.py:373
  (3 shorter events, 0.0 us)
Async XLA Ops:
  0.0 1.5 %copy-start.1 = (bf16[3,2,96,1536]{3,2,1,0:T(8,128)(2,1)S(1)}, bf16[3,2,96,1536]{3,2,1,0:T(8,128)(2,1)}, u32[]{:S(2)}) copy-start(bf16[3,2,96,1536]{3,2,1,0:T(8,128)(2,1)} %param.7) | copy-start | bytes 5308420
  1.8 14.7 %collective-permute-start.3 = (bf16[6,16,1536]{2,1,0:T(8,128)(2,1)S(1)}, bf16[6,16,1536]{2,1,0:T(8,128)(2,1)S(1)}, u32[]{:S(2)}, u32[]{:S(2)}) collective-permute-start(bf16[6,16,1536]{2,1,0:T(8,128)(2,1)S(1)} %get-tuple-element.30), channel_id=1, source_target_pairs={{0,32},{32,64},{64,96},{96,0},{1,33},{33,65},{65,97},{97,1},{2,34}... | collective-permute-start | bytes 884744 | tf_op jit(solution)/shard_map/ppermute | solution.py:425
  3.9 15.2 %collective-permute-start.4 = (bf16[6,16,1536]{2,1,0:T(8,128)(2,1)S(1)}, bf16[6,16,1536]{2,1,0:T(8,128)(2,1)S(1)}, u32[]{:S(2)}, u32[]{:S(2)}) collective-permute-start(bf16[6,16,1536]{2,1,0:T(8,128)(2,1)S(1)} %get-tuple-element.31), channel_id=1, source_target_pairs={{0,64},{32,96},{64,0},{96,32},{1,65},{33,97},{65,1},{97,33},{2,66}... | collective-permute-start | bytes 884744 | tf_op jit(solution)/shard_map/ppermute | solution.py:425
  6.3 12.7 %collective-permute-start.5 = (bf16[6,16,1536]{2,1,0:T(8,128)(2,1)S(1)}, bf16[6,16,1536]{2,1,0:T(8,128)(2,1)S(1)}, u32[]{:S(2)}, u32[]{:S(2)}) collective-permute-start(bf16[6,16,1536]{2,1,0:T(8,128)(2,1)S(1)} %get-tuple-element.32), channel_id=1, source_target_pairs={{0,96},{32,0},{64,32},{96,64},{1,97},{33,1},{65,33},{97,65},{2,98}... | collective-permute-start | bytes 884744 | tf_op jit(solution)/shard_map/ppermute | solution.py:425
  7.5 6.4 %copy-start = (bf16[1,24,256,1536]{3,2,1,0:T(8,128)(2,1)S(1)}, bf16[1,24,256,1536]{3,2,1,0:T(8,128)(2,1)}, u32[]{:S(2)}) copy-start(bf16[1,24,256,1536]{3,2,1,0:T(8,128)(2,1)} %param.8) | copy-start | bytes 56623108
  13.9 5.2 %copy-start.3 = (s32[3072]{0:T(1024)S(1)}, s32[3072]{0:T(1024)}, u32[]{:S(2)}) copy-start(s32[3072]{0:T(1024)} %orders_ref.5) | copy-start | bytes 36868
  15.2 8.6 %collective-permute-start = (bf16[6,8,1536]{2,1,0:T(8,128)(2,1)S(1)}, bf16[6,8,1536]{2,1,0:T(8,128)(2,1)S(1)}, u32[]{:S(2)}, u32[]{:S(2)}) collective-permute-start(bf16[6,8,1536]{2,1,0:T(8,128)(2,1)S(1)} %get-tuple-element.25), channel_id=1, source_target_pairs={{0,32},{32,64},{64,96},{96,0},{1,33},{33,65},{65,97},{97,1},{2,34}... | collective-permute-start | bytes 442376 | tf_op jit(solution)/shard_map/ppermute | solution.py:425
  15.6 9.8 %collective-permute-start.1 = (bf16[6,8,1536]{2,1,0:T(8,128)(2,1)S(1)}, bf16[6,8,1536]{2,1,0:T(8,128)(2,1)S(1)}, u32[]{:S(2)}, u32[]{:S(2)}) collective-permute-start(bf16[6,8,1536]{2,1,0:T(8,128)(2,1)S(1)} %get-tuple-element.26), channel_id=1, source_target_pairs={{0,64},{32,96},{64,0},{96,32},{1,65},{33,97},{65,1},{97,33},{2,66}... | collective-permute-start | bytes 442376 | tf_op jit(solution)/shard_map/ppermute | solution.py:425
  16.4 8.9 %collective-permute-start.2 = (bf16[6,8,1536]{2,1,0:T(8,128)(2,1)S(1)}, bf16[6,8,1536]{2,1,0:T(8,128)(2,1)S(1)}, u32[]{:S(2)}, u32[]{:S(2)}) collective-permute-start(bf16[6,8,1536]{2,1,0:T(8,128)(2,1)S(1)} %get-tuple-element.27), channel_id=1, source_target_pairs={{0,96},{32,0},{64,32},{96,64},{1,97},{33,1},{65,33},{97,65},{2,98}... | collective-permute-start | bytes 442376 | tf_op jit(solution)/shard_map/ppermute | solution.py:425
  19.1 21.2 %copy-start.6 = (s32[4,16]{1,0:T(4,128)S(1)}, s32[4,16]{1,0:T(4,128)}, u32[]{:S(2)}) copy-start(s32[4,16]{1,0:T(4,128)} %lens_ref.1) | copy-start | bytes 772
  19.1 36.1 %copy-start.2 = (bf16[256,256]{1,0:T(8,128)(2,1)S(1)}, bf16[256,256]{1,0:T(8,128)(2,1)}, u32[]{:S(2)}) copy-start(bf16[256,256]{1,0:T(8,128)(2,1)} %constant.8.clone.stage2_ref) | copy-start | bytes 393220
  19.1 36.1 %copy-start.4 = (bf16[128,144]{1,0:T(8,128)(2,1)S(1)}, bf16[128,144]{1,0:T(8,128)(2,1)}, u32[]{:S(2)}) copy-start(bf16[128,144]{1,0:T(8,128)(2,1)} %constant.6.clone.stage1_ref) | copy-start | bytes 110596
  19.1 36.1 %copy-start.5 = (f32[128,128]{1,0:T(8,128)S(1)}, f32[128,128]{1,0:T(8,128)}, u32[]{:S(2)}) copy-start(f32[128,128]{1,0:T(8,128)} %constant.7.clone.twiddle_ref) | copy-start | bytes 196612
  29.1 26.1 %all-to-all-start = ((s32[128,1,1280]{2,1,0:T(1,128)}), s32[128,1,1280]{2,1,0:T(1,128)S(1)}, u32[]{:S(2)}, u32[]{:S(2)}) async-start(s32[128,1,1280]{2,1,0:T(1,128)} %bitcast.2), calls=%async_computation | async-start | bytes 1310720 | tf_op jit(solution)/shard_map/all_to_all | solution.py:438
